TPU v7x, 256 devices: a whole 4x4x8 slice. The times are simulated.
256 devices in a mesh: event: 16 (over x_hi, z), lon: 16 (over y, x_lo, core).
Axes of the slice: x: 4 (x_hi: 2, x_lo: 2; x = x_hi * 2 + x_lo), y: 4, z: 8, core: 2. Of those that a mesh axis runs over, the one named last changes fastest.
Arguments:
- adjoint_init: bfloat16 [16, 9, 16, 512, 128], P('event', None, None, 'lon'), may hold values from -6 to 6
- forward_state: bfloat16 [16, 8, 9, 16, 512, 128], P('event', None, None, None, 'lon'), may hold values from -3 to 3
- p_speed: float32 [16, 512, 128], P(None, 'lon'), may hold values from 0.3 to 0.5
- s_speed: float32 [16, 512, 128], P(None, 'lon'), may hold values from 0.1 to 0.2
- density: float32 [16, 512, 128], P(None, 'lon'), may hold values from 0.8 to 1.6
Outputs:
- kernels: float32 [3, 16, 512, 128], P(None, 'event', 'lon')
All inputs are finite; a program needn't handle non-finite values.
Results may differ from a plain program's by a relative error of at most 0.015.
Values may be sent and summed in bfloat16 or wider, within the bound.
No kernel may reach another device: no remote copies, remote signals or barrier semaphores. Data moves between devices by JAX's collectives and lax.ppermute only.
A program may use at most 64 MiB of HBM per device.

v0:
```python
import functools

import jax
import jax.numpy as jnp
from jax import lax
from jax.experimental import pallas as pl
from jax.experimental.pallas import tpu as pltpu
from jax.sharding import PartitionSpec as P

F32, BF16 = jnp.float32, jnp.bfloat16
HALO = 8
VX, VY, VZ, XX, YY, ZZ, XY, XZ, YZ = range(9)
LAME, SHEAR2, BUOY = range(3)


def propagate(steps, levels, width, init, left, right, coef, forward, out, state, mat, sums):
    wide = width + 2 * HALO
    step = pl.program_id(0)
    lane = lax.broadcasted_iota(jnp.int32, (8, 128), 1)
    row_chunks = [(HALO, 8, None)]
    row_chunks += [(2 * HALO + start, 16, start) for start in range(0, width, 16)]
    row_chunks += [(2 * HALO + width, 8, None)]

    @pl.when(step == 0)
    def _():
        zero_level = jnp.zeros((9, 1, wide + 16, 128), F32)
        state[:, pl.ds(0, 1)] = zero_level
        state[:, pl.ds(levels + 1, 1)] = zero_level

        def load(level, carry):
            for field in range(9):
                state[field, level + 1, pl.ds(0, 8)] = jnp.zeros((8, 128), F32)
                state[field, level + 1, pl.ds(wide + 8, 8)] = jnp.zeros((8, 128), F32)
                state[field, level + 1, pl.ds(8, HALO)] = left[field, level].astype(F32)
                state[field, level + 1, pl.ds(8 + HALO, width)] = init[field, level].astype(F32)
                state[field, level + 1, pl.ds(8 + HALO + width, HALO)] = right[field, level].astype(F32)
            for which in range(3):
                mat[which, level, pl.ds(0, HALO)] = left[9 + which, level].astype(F32)
                mat[which, level, pl.ds(HALO, width)] = coef[which, level]
                mat[which, level, pl.ds(HALO + width, HALO)] = right[9 + which, level].astype(F32)
                sums[which, level] = jnp.zeros((width, 128), F32)
            return carry

        lax.fori_loop(0, levels, load, 0)

    def before_lat(value):
        edge = lax.broadcasted_iota(jnp.int32, value.shape, 1) == 0
        return jnp.where(edge, 0.0, pltpu.roll(value, 1, 1))

    def after_lat(value):
        edge = lax.broadcasted_iota(jnp.int32, value.shape, 1) == 127
        return jnp.where(edge, 0.0, pltpu.roll(value, 127, 1))

    def rounded(value):
        return value.astype(BF16).astype(F32)

    def velocity(level):
        for start, rows, own in row_chunks:
            def at(field, lev=0, lon=0):
                return state[field, level + 1 + lev, pl.ds(start + lon, rows)]

            xx, yy, zz, xy, xz, yz = [at(field) for field in range(3, 9)]
            force_x = (at(XX, lon=1) - xx) + (xy - before_lat(xy)) + (xz - at(XZ, lev=-1))
            force_y = (xy - at(XY, lon=-1)) + (after_lat(yy) - yy) + (yz - at(YZ, lev=-1))
            force_z = (xz - at(XZ, lon=-1)) + (yz - before_lat(yz)) + (at(ZZ, lev=1) - zz)
            buoy = mat[BUOY, level, pl.ds(start - 8, rows)]
            for field, force in ((VX, force_x), (VY, force_y), (VZ, force_z)):
                state[field, level + 1, pl.ds(start, rows)] = rounded(at(field) + buoy * force)

    def stress(level):
        for start, rows, own in row_chunks:
            def at(field, lev=0, lon=0):
                return state[field, level + 1 + lev, pl.ds(start + lon, rows)]

            vx, vy, vz = at(VX), at(VY), at(VZ)
            e_xx = vx - at(VX, lon=-1)
            e_yy = vy - before_lat(vy)
            e_zz = vz - at(VZ, lev=-1)
            d_xy = (after_lat(vx) - vx) + (at(VY, lon=1) - vy)
            d_xz = (at(VX, lev=1) - vx) + (at(VZ, lon=1) - vz)
            d_yz = (at(VY, lev=1) - vy) + (after_lat(vz) - vz)
            trace = e_xx + e_yy + e_zz
            lame = mat[LAME, level, pl.ds(start - 8, rows)]
            shear2 = mat[SHEAR2, level, pl.ds(start - 8, rows)]
            shear = 0.5 * shear2
            volume = lame * trace
            for field, change in (
                (XX, volume + shear2 * e_xx),
                (YY, volume + shear2 * e_yy),
                (ZZ, volume + shear2 * e_zz),
                (XY, shear * d_xy),
                (XZ, shear * d_xz),
                (YZ, shear * d_yz),
            ):
                state[field, level + 1, pl.ds(start, rows)] = rounded(at(field) + change)
            if own is not None:
                f = [forward[0, 0, field, level, pl.ds(own, rows)].astype(F32) for field in range(9)]
                mine = pl.ds(own, rows)
                sums[0, level, mine] += trace * (f[3] + f[4] + f[5])
                sums[1, level, mine] += (e_xx * f[3] + e_yy * f[4] + e_zz * f[5]) + (
                    d_xy * f[6] + d_xz * f[7] + d_yz * f[8]
                )
                sums[2, level, mine] += vx * f[0] + vy * f[1] + vz * f[2]

    velocity(0)

    def sweep(level, carry):
        velocity(level + 1)
        stress(level)
        return carry

    lax.fori_loop(0, levels - 1, sweep, 0)
    stress(levels - 1)

    @pl.when(step == steps - 1)
    def _():
        def store(level, carry):
            out[level, 0] = sums[0, level].astype(BF16)
            out[level, 1] = (2.0 * sums[1, level]).astype(BF16)
            out[level, 2] = sums[2, level].astype(BF16)
            return carry

        lax.fori_loop(0, levels, store, 0)


def run_steps(init, left, right, coef, forward):
    _, steps, _, levels, width, lat = forward.shape
    wide = width + 2 * HALO
    whole = lambda array: pl.BlockSpec(array.shape, lambda t, n=array.ndim: (0,) * n)
    return pl.pallas_call(
        functools.partial(propagate, steps, levels, width),
        grid=(steps,),
        in_specs=[
            whole(init),
            whole(left),
            whole(right),
            whole(coef),
            pl.BlockSpec((1, 1, 9, levels, width, lat), lambda t: (0, t, 0, 0, 0, 0)),
        ],
        out_specs=pl.BlockSpec((levels, 3, width, lat), lambda t: (0, 0, 0, 0)),
        out_shape=jax.ShapeDtypeStruct((levels, 3, width, lat), BF16),
        scratch_shapes=[
            pltpu.VMEM((9, levels + 2, wide + 16, lat), F32),
            pltpu.VMEM((3, levels, wide, lat), F32),
            pltpu.VMEM((3, levels, width, lat), F32),
        ],
        compiler_params=pltpu.CompilerParams(vmem_limit_bytes=48 * 1024 * 1024),
    )(init, left, right, coef, forward)


def combine_kernels(total, p_speed, s_speed, density):
    lame = density * (p_speed * p_speed - 2.0 * s_speed * s_speed)
    shear = density * s_speed * s_speed
    return jnp.stack(
        [
            2.0 * density * p_speed * p_speed * total[0],
            2.0 * density * s_speed * s_speed * (total[1] - 2.0 * total[0]),
            density * total[2] + lame * total[0] + shear * total[1],
        ]
    )


def shards(adjoint_init, forward_state, p_speed, s_speed, density):
    init = adjoint_init[0]
    width = init.shape[2]
    lame = density * (p_speed * p_speed - 2.0 * s_speed * s_speed)
    shear2 = 2.0 * density * s_speed * s_speed
    coef = jnp.stack([lame, shear2, 1.0 / density])

    def edge(start):
        return jnp.concatenate(
            [init[:, :, start : start + HALO], coef[:, :, start : start + HALO].astype(BF16)]
        )

    count = lax.axis_size("lon")
    up = [(i, (i + 1) % count) for i in range(count)]
    left = lax.ppermute(edge(width - HALO), "lon", up)
    right = lax.ppermute(edge(0), "lon", [(j, i) for i, j in up])
    partial = run_steps(init, left, right, coef, forward_state)
    parts = lax.all_to_all(partial, "event", 0, 0, tiled=True)
    total = jnp.sum(parts.astype(F32), axis=0, keepdims=False)[:, None]
    first_row = lax.axis_index("event")
    own = [lax.dynamic_slice_in_dim(item, first_row, 1, 0) for item in (p_speed, s_speed, density)]
    return combine_kernels(total, *own)


def solution(mesh):
    placed = (
        P("event", None, None, "lon", None),
        P("event", None, None, None, "lon", None),
        P(None, "lon", None),
        P(None, "lon", None),
        P(None, "lon", None),
    )
    return jax.shard_map(
        shards, mesh=mesh, in_specs=placed, out_specs=P(None, "event", "lon", None), check_vma=False
    )
```

profile of v0, /device:TPU:8, one launch (start us, length us, event | category | flops | bytes accessed | tf_op | source)
XLA Modules:
  0.0 63.0 jit_solution(11115080800426972391)
XLA Ops:
  0.0 1.2 %fusion.2 = (f32[1,16,32,128]{3,2,1,0:T(8,128)S(1)}, f32[1,16,32,128]{3,2,1,0:T(8,128)S(1)}, f32[1,16,32,128]{3,2,1,0:T(8,128)S(1)}) fusion(f32[16,32,128]{2,1,0:T(8,128)} %param.9, f32[16,32,128]{2,1,0:T(8,128)} %param.8, f32[16,32,128]{2,1,0:T(8,128)} %param.7), kind=kLoop, calls=%fused_computation.8 | loop fusion | flops 589824 | bytes 1572864 | tf_op jit(solution)/shard_map/stack | solution.py:168
  1.2 0.0 copy-start
  1.2 0.1 fusion.15
  1.3 1.2 %copy-done = bf16[1,9,16,32,128]{4,3,2,1,0:T(8,128)(2,1)S(1)} copy-done((bf16[1,9,16,32,128]{4,3,2,1,0:T(8,128)(2,1)S(1)}, bf16[1,9,16,32,128]{4,3,2,1,0:T(8,128)(2,1)}, u32[]{:S(2)}) %copy-start) | copy-done | bytes 1179672
  2.5 0.1 fusion.16
  2.7 0.1 collective-permute-start
  2.8 2.7 %collective-permute-start.1 = (bf16[12,16,8,128]{3,2,1,0:T(8,128)(2,1)S(1)}, bf16[12,16,8,128]{3,2,1,0:T(8,128)(2,1)S(1)}, u32[]{:S(2)}, u32[]{:S(2)}) collective-permute-start(bf16[12,16,8,128]{3,2,1,0:T(8,128)(2,1)S(1)} %pad_maximum_fusion.2), channel_id=1, source_target_pairs={{1,0},{2,1},{3,2},{4,3},{5,4},{6,5},{7,6},{8,7},{9,8},{10,9},{11,1... | collective-permute-start | bytes 1179656 | tf_op jit(solution)/shard_map/ppermute | solution.py:178
  5.5 0.1 pad_maximum_fusion.coef
  5.6 8.6 %collective-permute-done.left = bf16[12,16,8,128]{3,2,1,0:T(8,128)(2,1)S(1)} collective-permute-done((bf16[12,16,8,128]{3,2,1,0:T(8,128)(2,1)S(1)}, bf16[12,16,8,128]{3,2,1,0:T(8,128)(2,1)S(1)}, u32[]{:S(2)}, u32[]{:S(2)}) %collective-permute-start) | collective-permute-done | bytes 393248 | tf_op jit(solution)/shard_map/ppermute | solution.py:177
  14.2 0.0 collective-permute-done.1.right
  14.2 20.9 %shard_map.55 = bf16[16,3,32,128]{3,2,1,0:T(8,128)(2,1)} custom-call(bf16[9,16,32,128]{3,2,1,0:T(8,128)(2,1)S(1)} %bitcast.14, bf16[12,16,8,128]{3,2,1,0:T(8,128)(2,1)S(1)} %collective-permute-done.left, bf16[12,16,8,128]{3,2,1,0:T(8,128)(2,1)S(1)} %collective-permute-done.1.right, f32[3,16,32,128]{3,2,1,0:T(8,128)S(1)} %pad_maximum_fusion.coef, ...), custom_call_target="tpu_custom_call" | custom-call | tf_op jit(solution)/shard_map/pallas_call | solution.py:130
  35.2 11.4 %all-to-all-start = ((bf16[16,3,32,128]{3,2,1,0:T(8,128)(2,1)}), bf16[16,3,32,128]{3,2,1,0:T(8,128)(2,1)S(1)}, u32[]{:S(2)}, u32[]{:S(2)}) async-start(bf16[16,3,32,128]{3,2,1,0:T(8,128)(2,1)} %shard_map.55), calls=%async_computation | async-start | bytes 786432 | tf_op jit(solution)/shard_map/all_to_all | solution.py:180
  46.5 15.0 %all-to-all-done = bf16[16,3,32,128]{3,2,1,0:T(8,128)(2,1)S(1)} async-done(((bf16[16,3,32,128]{3,2,1,0:T(8,128)(2,1)}), bf16[16,3,32,128]{3,2,1,0:T(8,128)(2,1)S(1)}, u32[]{:S(2)}, u32[]{:S(2)}) %all-to-all-start) | async-done | bytes 393248 | tf_op jit(solution)/shard_map/all_to_all | solution.py:180
  61.6 0.1 convert_reduce_fusion
  61.6 0.8 %fusion.5 = (f32[1,1,32,128]{3,2,1,0:T(8,128)S(1)}, f32[1,1,32,128]{3,2,1,0:T(8,128)S(1)}, f32[1,1,32,128]{3,2,1,0:T(8,128)S(1)}) fusion(f32[16,32,128]{2,1,0:T(8,128)} %param.7, s32[]{:T(128)S(6)} %select_n.2, f32[3,32,128]{2,1,0:T(8,128)S(1)} %convert_reduce_fusion, f32[16,32,128]{2,1,0:T(8,128)} %param.9, f32[16,32,128]{2,1,0:T(8,128)} %param.8), kind=kLoop, calls=%fused_computation.17 | loop fusion | flops 86016 | bytes 147460 | tf_op jit(solution)/shard_map/stack | solution.py:154
  62.4 0.6 pad_maximum_fusion.3
  (3 shorter events, 0.1 us)
Async XLA Ops:
  1.2 1.3 %copy-start = (bf16[1,9,16,32,128]{4,3,2,1,0:T(8,128)(2,1)S(1)}, bf16[1,9,16,32,128]{4,3,2,1,0:T(8,128)(2,1)}, u32[]{:S(2)}) copy-start(bf16[1,9,16,32,128]{4,3,2,1,0:T(8,128)(2,1)} %param.5) | copy-start | bytes 3538948
  2.7 11.5 %collective-permute-start = (bf16[12,16,8,128]{3,2,1,0:T(8,128)(2,1)S(1)}, bf16[12,16,8,128]{3,2,1,0:T(8,128)(2,1)S(1)}, u32[]{:S(2)}, u32[]{:S(2)}) collective-permute-start(bf16[12,16,8,128]{3,2,1,0:T(8,128)(2,1)S(1)} %pad_maximum_fusion.1), channel_id=1, source_target_pairs={{0,1},{1,2},{2,3},{3,4},{4,5},{5,6},{6,7},{7,8},{8,9},{9,10},{10,1... | collective-permute-start | bytes 1179656 | tf_op jit(solution)/shard_map/ppermute | solution.py:177
  2.8 11.4 %collective-permute-start.1 = (bf16[12,16,8,128]{3,2,1,0:T(8,128)(2,1)S(1)}, bf16[12,16,8,128]{3,2,1,0:T(8,128)(2,1)S(1)}, u32[]{:S(2)}, u32[]{:S(2)}) collective-permute-start(bf16[12,16,8,128]{3,2,1,0:T(8,128)(2,1)S(1)} %pad_maximum_fusion.2), channel_id=1, source_target_pairs={{1,0},{2,1},{3,2},{4,3},{5,4},{6,5},{7,6},{8,7},{9,8},{10,9},{11,1... | collective-permute-start | bytes 1179656 | tf_op jit(solution)/shard_map/ppermute | solution.py:178
  35.2 26.4 %all-to-all-start = ((bf16[16,3,32,128]{3,2,1,0:T(8,128)(2,1)}), bf16[16,3,32,128]{3,2,1,0:T(8,128)(2,1)S(1)}, u32[]{:S(2)}, u32[]{:S(2)}) async-start(bf16[16,3,32,128]{3,2,1,0:T(8,128)(2,1)} %shard_map.55), calls=%async_computation | async-start | bytes 786432 | tf_op jit(solution)/shard_map/all_to_all | solution.py:180
where the time goes:
time: 63.4 us; the launch traced here: 63 us
  waiting for transfers between devices  23.7 us (37%)
  Pallas kernels  20.9 us (33%)
  starting transfers between devices  14.2 us (22%)
  other arithmetic  2.86 us (5%)
  local copies, waits for them, and re-layouts  1.34 us (2%)
    pallas_call x1, Pallas kernels, run_steps(): pl.pallas_call(functools.partial(propagate, steps, levels, width), grid=(...  20.9 us
    all_to_all x1, waiting for transfers between devices, shards(): parts = lax.all_to_all(partial, 'event', 0, 0, tiled=True)  15 us
    all_to_all x1, starting transfers between devices, shards(): parts = lax.all_to_all(partial, 'event', 0, 0, tiled=True)  11.4 us
    ppermute x1, waiting for transfers between devices, shards(): left = lax.ppermute(edge(width - HALO), 'lon', up)  8.62 us
    ppermute x1, starting transfers between devices, shards(): right = lax.ppermute(edge(0), 'lon', [(j, i) for i, j in up])  2.7 us
    another operation x2, other arithmetic, combine_kernels(): jnp.stack([2.0 * density * p_speed * p_speed * total[0], 2.0 * density *...  1.4 us
    another operation x2, other arithmetic, shards(): coef = jnp.stack([lame, shear2, 1.0 / density])  1.27 us
  transfers between devices with their start and end apart: 3, of which 2 were waited for; matrix products, arithmetic and copies ran while one was open for 0% of the time, Pallas kernels for 0%

commit v1 on v0

v1 whole, which is shorter than its diff:
```python
import functools

import jax
import jax.numpy as jnp
from jax import lax
from jax.experimental import pallas as pl
from jax.experimental.pallas import tpu as pltpu
from jax.sharding import PartitionSpec as P

F32, BF16 = jnp.float32, jnp.bfloat16
HALO = 8
PAD = 8
VX, VY, VZ, XX, YY, ZZ, XY, XZ, YZ = range(9)
LAME, SHEAR2, BUOY = range(3)


def before_lat(value):
    edge = lax.broadcasted_iota(jnp.int32, value.shape, 1) == 0
    return jnp.where(edge, 0.0, pltpu.roll(value, 1, 1))


def after_lat(value):
    edge = lax.broadcasted_iota(jnp.int32, value.shape, 1) == 127
    return jnp.where(edge, 0.0, pltpu.roll(value, 127, 1))


def rounded(value):
    return value.astype(BF16).astype(F32)


def push(at, put, buoy):
    x_buoy, shift, yz_buoy = buoy
    xy, xz = at(XY, 0, shift), at(XZ, 0, shift)
    xy_x, xz_x = at(XY, 0, 0), at(XZ, 0, 0)
    yz = at(YZ, 0, shift)
    force_x = (at(XX, 0, 1) - at(XX, 0, 0)) + (xy_x - before_lat(xy_x)) + (xz_x - at(XZ, -1, 0))
    yy = at(YY, 0, shift)
    force_y = (xy - at(XY, 0, shift - 1)) + (after_lat(yy) - yy) + (yz - at(YZ, -1, shift))
    force_z = (
        (xz - at(XZ, 0, shift - 1))
        + (yz - before_lat(yz))
        + (at(ZZ, 1, shift) - at(ZZ, 0, shift))
    )
    put(VX, 0, rounded(at(VX, 0, 0) + x_buoy * force_x))
    put(VY, shift, rounded(at(VY, 0, shift) + yz_buoy * force_y))
    put(VZ, shift, rounded(at(VZ, 0, shift) + yz_buoy * force_z))


def strain(at, put, lame, shear2):
    vx, vy, vz = at(VX, 0, 0), at(VY, 0, 0), at(VZ, 0, 0)
    e_xx = vx - at(VX, 0, -1)
    e_yy = vy - before_lat(vy)
    e_zz = vz - at(VZ, -1, 0)
    d_xy = (after_lat(vx) - vx) + (at(VY, 0, 1) - vy)
    d_xz = (at(VX, 1, 0) - vx) + (at(VZ, 0, 1) - vz)
    d_yz = (at(VY, 1, 0) - vy) + (after_lat(vz) - vz)
    trace = e_xx + e_yy + e_zz
    shear = 0.5 * shear2
    volume = lame * trace
    for field, change in (
        (XX, volume + shear2 * e_xx),
        (YY, volume + shear2 * e_yy),
        (ZZ, volume + shear2 * e_zz),
        (XY, shear * d_xy),
        (XZ, shear * d_xz),
        (YZ, shear * d_yz),
    ):
        put(field, 0, rounded(at(field, 0, 0) + change))
    return (vx, vy, vz), (e_xx, e_yy, e_zz, d_xy, d_xz, d_yz), trace


def terms(speed, rate, trace, f):
    return (
        trace * (f[3] + f[4] + f[5]),
        (rate[0] * f[3] + rate[1] * f[4] + rate[2] * f[5])
        + (rate[3] * f[6] + rate[4] * f[7] + rate[5] * f[8]),
        speed[0] * f[0] + speed[1] * f[1] + speed[2] * f[2],
    )


def inner(steps, levels, width, init, coef, forward, sums, stair, state):
    step = pl.program_id(0)

    def keep(level, side, field, row, value):
        stair[side, field, level, pl.ds(row, 1)] = value

    @pl.when(step == 0)
    def _():
        empty = jnp.zeros((9, 1, width + 2 * PAD, 128), F32)
        state[:, pl.ds(0, 1)] = empty
        state[:, pl.ds(levels + 1, 1)] = empty

        def load(level, carry):
            for field in range(9):
                state[field, level + 1, pl.ds(0, PAD)] = jnp.zeros((PAD, 128), F32)
                state[field, level + 1, pl.ds(PAD + width, PAD)] = jnp.zeros((PAD, 128), F32)
                state[field, level + 1, pl.ds(PAD, width)] = init[field, level].astype(F32)
                stair[0, field, level] = jnp.zeros((16, 128), F32)
                stair[1, field, level] = jnp.zeros((16, 128), F32)
                if field != VX:
                    stair[0, field, level, pl.ds(0, 1)] = state[field, level + 1, pl.ds(PAD, 1)]
                if field not in (VY, VZ):
                    stair[1, field, level, pl.ds(15, 1)] = state[field, level + 1, pl.ds(PAD + width - 1, 1)]
            for which in range(3):
                sums[which, level] = jnp.zeros((width, 128), F32)
            return carry

        lax.fori_loop(0, levels, load, 0)

    def view(level, start, rows):
        def at(field, lev, lon):
            return state[field, level + 1 + lev, pl.ds(PAD + start + lon, rows)]

        def put(field, lon, value):
            state[field, level + 1, pl.ds(PAD + start + lon, rows)] = value

        return at, put

    def velocity(level):
        for start in range(0, width, 16):
            buoy = coef[BUOY, level, pl.ds(start, 16)]
            push(*view(level, start, 16), (buoy, 0, buoy))
        for field in (VX, VY, VZ):
            first = step if field == VX else step + 1
            last = 30 - step if field == VX else 31 - step
            keep(level, 0, field, first, state[field, level + 1, pl.ds(PAD + first, 1)])
            keep(level, 1, field, last - 16, state[field, level + 1, pl.ds(PAD + last, 1)])

    def stress(level):
        for start in range(0, width, 16):
            mine = pl.ds(start, 16)
            parts = strain(*view(level, start, 16), coef[LAME, level, mine], coef[SHEAR2, level, mine])
            f = [forward[0, 0, field, level, mine].astype(F32) for field in range(9)]
            column = start + lax.broadcasted_iota(jnp.int32, (16, 128), 0)
            right = (column > step) & (column < width - 1 - step)
            for which, term in enumerate(terms(*parts, f)):
                sums[which, level, mine] += jnp.where(right, term, 0.0)
        for field in range(3, 9):
            keep(level, 0, field, step + 1, state[field, level + 1, pl.ds(PAD + step + 1, 1)])
            keep(level, 1, field, 14 - step, state[field, level + 1, pl.ds(PAD + 30 - step, 1)])

    velocity(0)
    for level in range(levels):
        if level + 1 < levels:
            velocity(level + 1)
        stress(level)


def outer(steps, levels, width, left, right, coef, forward, first_sums, stair, out, state, mat, sums, wide_f):
    step = pl.program_id(0)

    @pl.when(step == 0)
    def _():
        for side in range(2):
            empty = jnp.zeros((9, 1, 24, 128), F32)
            state[side, :, pl.ds(0, 1)] = empty
            state[side, :, pl.ds(levels + 1, 1)] = empty

        def load(level, carry):
            for field in range(9):
                halo = left[field, level].astype(F32)
                state[0, field, level + 1, pl.ds(8, 16)] = stair[0, field, level]
                state[0, field, level + 1, pl.ds(0, 8)] = halo
                state[1, field, level + 1, pl.ds(0, 16)] = stair[1, field, level]
                state[1, field, level + 1, pl.ds(16, 8)] = right[field, level].astype(F32)
                wide_f[0, field, level, pl.ds(0, 8)] = jnp.zeros((8, 128), F32)
                wide_f[1, field, level, pl.ds(8, 8)] = jnp.zeros((8, 128), F32)
            for which in range(3):
                mat[0, which, level, pl.ds(0, 8)] = left[9 + which, level].astype(F32)
                mat[0, which, level, pl.ds(8, 16)] = coef[which, level, pl.ds(0, 16)]
                mat[1, which, level, pl.ds(0, 16)] = coef[which, level, pl.ds(width - 16, 16)]
                mat[1, which, level, pl.ds(16, 8)] = right[9 + which, level].astype(F32)
                sums[which, level, pl.ds(0, 8)] = jnp.zeros((8, 128), F32)
                sums[which, level, pl.ds(8, width)] = first_sums[which, level]
                sums[which, level, pl.ds(8 + width, 8)] = jnp.zeros((8, 128), F32)
            return carry

        lax.fori_loop(0, levels, load, 0)

    places = ((step, step + 1, step + 1), (15 - step, 15 - step, 39 - step))

    def view(side, level, start):
        def at(field, lev, lon):
            return state[side, field, level + 1 + lev, pl.ds(start + lon, 8)]

        def put(field, lon, value):
            state[side, field, level + 1, pl.ds(start + lon, 8)] = value

        return at, put

    def velocity(level):
        for side in range(2):
            start = places[side][0]
            x_buoy = mat[side, BUOY, level, pl.ds(start, 8)]
            yz_buoy = mat[side, BUOY, level, pl.ds(start + 1, 8)]
            push(*view(side, level, start), (x_buoy, 1, yz_buoy))

    def stress(level):
        for side in range(2):
            _, start, place = places[side]
            rows = pl.ds(start, 8)
            parts = strain(*view(side, level, start), mat[side, LAME, level, rows], mat[side, SHEAR2, level, rows])
            own = pl.ds(0, 16) if side == 0 else pl.ds(width - 16, 16)
            for field in range(9):
                value = forward[0, 0, field, level, own].astype(F32)
                if side == 0:
                    wide_f[side, field, level, pl.ds(8, 8)] = value[:8]
                else:
                    wide_f[side, field, level, pl.ds(0, 8)] = value[8:]
            where_f = step + 1 if side == 0 else 7 - step
            f = [wide_f[side, field, level, pl.ds(where_f, 8)] for field in range(9)]
            for which, term in enumerate(terms(*parts, f)):
                sums[which, level, pl.ds(place, 8)] += term

    velocity(0)
    for level in range(levels):
        if level + 1 < levels:
            velocity(level + 1)
        stress(level)

    @pl.when(step == steps - 1)
    def _():
        def store(level, carry):
            for which, factor in enumerate((1.0, 2.0, 1.0)):
                out[level, which] = (factor * sums[which, level, pl.ds(8, width)]).astype(BF16)
            return carry

        lax.fori_loop(0, levels, store, 0)


def whole(array):
    return pl.BlockSpec(array.shape, lambda t, n=len(array.shape): (0,) * n)


def run_inner(init, coef, forward):
    _, steps, _, levels, width, lat = forward.shape
    outs = [
        jax.ShapeDtypeStruct((3, levels, width, lat), F32),
        jax.ShapeDtypeStruct((2, 9, levels, 16, lat), F32),
    ]
    return pl.pallas_call(
        functools.partial(inner, steps, levels, width),
        grid=(steps,),
        in_specs=[
            whole(init),
            whole(coef),
            pl.BlockSpec((1, 1, 9, levels, width, lat), lambda t: (0, t, 0, 0, 0, 0)),
        ],
        out_specs=[whole(item) for item in outs],
        out_shape=outs,
        scratch_shapes=[pltpu.VMEM((9, levels + 2, width + 2 * PAD, lat), F32)],
        compiler_params=pltpu.CompilerParams(vmem_limit_bytes=30 * 1024 * 1024),
        cost_estimate=pl.CostEstimate(flops=60_000_000, bytes_accessed=30_000_000, transcendentals=0),
    )(init, coef, forward)


def run_outer(left, right, coef, forward, first_sums, stair):
    _, steps, _, levels, width, lat = forward.shape
    out = jax.ShapeDtypeStruct((levels, 3, width, lat), BF16)
    return pl.pallas_call(
        functools.partial(outer, steps, levels, width),
        grid=(steps,),
        in_specs=[
            whole(left),
            whole(right),
            whole(coef),
            pl.BlockSpec((1, 1, 9, levels, width, lat), lambda t: (0, t, 0, 0, 0, 0)),
            whole(first_sums),
            whole(stair),
        ],
        out_specs=whole(out),
        out_shape=out,
        scratch_shapes=[
            pltpu.VMEM((2, 9, levels + 2, 24, lat), F32),
            pltpu.VMEM((2, 3, levels, 24, lat), F32),
            pltpu.VMEM((3, levels, width + 16, lat), F32),
            pltpu.VMEM((2, 9, levels, 16, lat), F32),
        ],
        compiler_params=pltpu.CompilerParams(vmem_limit_bytes=40 * 1024 * 1024),
        cost_estimate=pl.CostEstimate(flops=30_000_000, bytes_accessed=20_000_000, transcendentals=0),
    )(left, right, coef, forward, first_sums, stair)


def combine_kernels(total, p_speed, s_speed, density):
    lame = density * (p_speed * p_speed - 2.0 * s_speed * s_speed)
    shear = density * s_speed * s_speed
    return jnp.stack(
        [
            2.0 * density * p_speed * p_speed * total[0],
            2.0 * density * s_speed * s_speed * (total[1] - 2.0 * total[0]),
            density * total[2] + lame * total[0] + shear * total[1],
        ]
    )


def shards(adjoint_init, forward_state, p_speed, s_speed, density):
    init = adjoint_init[0]
    width = init.shape[2]
    lame = density * (p_speed * p_speed - 2.0 * s_speed * s_speed)
    shear2 = 2.0 * density * s_speed * s_speed
    coef = jnp.stack([lame, shear2, 1.0 / density])

    def edge(start):
        return jnp.concatenate(
            [init[:, :, start : start + HALO], coef[:, :, start : start + HALO].astype(BF16)]
        )

    count = lax.axis_size("lon")
    up = [(i, (i + 1) % count) for i in range(count)]
    left = lax.ppermute(edge(width - HALO), "lon", up)
    right = lax.ppermute(edge(0), "lon", [(j, i) for i, j in up])
    first_sums, stair = run_inner(init, coef, forward_state)
    partial = run_outer(left, right, coef, forward_state, first_sums, stair)
    parts = lax.all_to_all(partial, "event", 0, 0, tiled=True)
    total = jnp.sum(parts.astype(F32), axis=0, keepdims=False)[:, None]
    first_row = lax.axis_index("event")
    own = [lax.dynamic_slice_in_dim(item, first_row, 1, 0) for item in (p_speed, s_speed, density)]
    return combine_kernels(total, *own)


def solution(mesh):
    placed = (
        P("event", None, None, "lon", None),
        P("event", None, None, None, "lon", None),
        P(None, "lon", None),
        P(None, "lon", None),
        P(None, "lon", None),
    )
    return jax.shard_map(
        shards, mesh=mesh, in_specs=placed, out_specs=P(None, "event", "lon", None), check_vma=False
    )
```

time: 63.4 us -> 88.5 us (1.40)
  the two profiles are of different devices: /device:TPU:8 before, /device:TPU:32 now
where the time goes in v1:
time: 88.5 us; the launch traced here: 88.1 us
  Pallas kernels  53.5 us (60%)
  starting transfers between devices  15 us (17%)
  waiting for transfers between devices  11.7 us (13%)
  local copies, waits for them, and re-layouts  4.82 us (5%)
  other arithmetic  2.86 us (3%)
    pallas_call x1, Pallas kernels, run_outer(): pl.pallas_call(functools.partial(outer, steps, levels, width), grid=(step...  43.2 us
    all_to_all x1, waiting for transfers between devices, shards(): parts = lax.all_to_all(partial, 'event', 0, 0, tiled=True)  11.7 us
    all_to_all x1, starting transfers between devices, shards(): parts = lax.all_to_all(partial, 'event', 0, 0, tiled=True)  11 us
    pallas_call x1, Pallas kernels, run_inner(): pl.pallas_call(functools.partial(inner, steps, levels, width), grid=(step...  10.3 us
    ppermute x1, starting transfers between devices, shards(): right = lax.ppermute(edge(0), 'lon', [(j, i) for i, j in up])  3.91 us
    unnamed x6, local copies, waits for them, and re-layouts  3.69 us
  transfers between devices with their start and end apart: 3, of which 1 were waited for; matrix products, arithmetic and copies ran while one was open for 0% of the time, Pallas kernels for 12%

profile of v1, /device:TPU:32, one launch (start us, length us, event | category | flops | bytes accessed | tf_op | source)
XLA Modules:
  0.0 88.1 jit_solution(11147399347944640652)
XLA Ops:
  0.0 1.1 %fusion.16 = (bf16[9,16,8,128]{3,2,1,0:T(8,128)(2,1)S(1)}, bf16[9,16,8,128]{3,2,1,0:T(8,128)(2,1)S(1)}) fusion(bf16[9,16,32,128]{3,2,1,0:T(8,128)(2,1)} %bitcast.13), kind=kLoop, calls=%fused_computation.29 | loop fusion | bytes 1179648 | tf_op jit(solution)/shard_map/slice | solution.py:305
  1.1 1.2 %fusion.2 = (f32[1,16,32,128]{3,2,1,0:T(8,128)S(1)}, f32[1,16,32,128]{3,2,1,0:T(8,128)S(1)}, f32[1,16,32,128]{3,2,1,0:T(8,128)S(1)}) fusion(f32[16,32,128]{2,1,0:T(8,128)} %param.9, f32[16,32,128]{2,1,0:T(8,128)} %param.8, f32[16,32,128]{2,1,0:T(8,128)} %param.7), kind=kLoop, calls=%fused_computation.8 | loop fusion | flops 589824 | bytes 1572864 | tf_op jit(solution)/shard_map/stack | solution.py:301
  2.3 0.0 copy-start.2
  2.4 0.1 fusion.15
  2.5 0.1 collective-permute-start
  2.6 3.9 %collective-permute-start.1 = (bf16[12,16,8,128]{3,2,1,0:T(8,128)(2,1)S(1)}, bf16[12,16,8,128]{3,2,1,0:T(8,128)(2,1)S(1)}, u32[]{:S(2)}, u32[]{:S(2)}) collective-permute-start(bf16[12,16,8,128]{3,2,1,0:T(8,128)(2,1)S(1)} %pad_maximum_fusion.2), channel_id=1, source_target_pairs={{1,0},{2,1},{3,2},{4,3},{5,4},{6,5},{7,6},{8,7},{9,8},{10,9},{11,1... | collective-permute-start | bytes 1179656 | tf_op jit(solution)/shard_map/ppermute | solution.py:311
  6.5 0.1 pad_maximum_fusion.coef
  6.6 0.0 copy-done.2
  6.6 0.0 copy-start
  6.6 3.7 %copy-done = bf16[1,8,9,16,32,128]{5,4,3,2,1,0:T(8,128)(2,1)S(1)} copy-done((bf16[1,8,9,16,32,128]{5,4,3,2,1,0:T(8,128)(2,1)S(1)}, bf16[1,8,9,16,32,128]{5,4,3,2,1,0:T(8,128)(2,1)}, u32[]{:S(2)}) %copy-start) | copy-done | bytes 9437208
  10.3 0.0 copy-start.1
  10.3 10.3 %shard_map.55 = (f32[3,16,32,128]{3,2,1,0:T(8,128)S(1)}, f32[2,9,16,16,128]{4,3,2,1,0:T(8,128)S(1)}) custom-call(bf16[9,16,32,128]{3,2,1,0:T(8,128)(2,1)S(1)} %bitcast.14, f32[3,16,32,128]{3,2,1,0:T(8,128)S(1)} %pad_maximum_fusion.coef, bf16[1,8,9,16,32,128]{5,4,3,2,1,0:T(8,128)(2,1)S(1)} %copy-done), custom_call_target="tpu_custom_call" | custom-call | flops 60000000 | bytes 30000000 | tf_op jit(solution)/shard_map/pallas_call | solution.py:241
  20.6 0.0 collective-permute-done.left
  20.6 0.0 collective-permute-done.1.right
  20.6 0.0 copy-done.1
  20.6 43.2 %shard_map.56 = bf16[16,3,32,128]{3,2,1,0:T(8,128)(2,1)} custom-call(bf16[12,16,8,128]{3,2,1,0:T(8,128)(2,1)S(1)} %collective-permute-done.left, bf16[12,16,8,128]{3,2,1,0:T(8,128)(2,1)S(1)} %collective-permute-done.1.right, f32[3,16,32,128]{3,2,1,0:T(8,128)S(1)} %pad_maximum_fusion.coef, bf16[1,8,9,16,32,128]{5,4,3,2,1,0:T(8,128)(2,1)S(1)} %copy-done.1, ...), custom_call_target="tpu_custom_call" | custom-call | flops 30000000 | bytes 20000000 | tf_op jit(solution)/shard_map/pallas_call | solution.py:260
  63.8 11.0 %all-to-all-start = ((bf16[16,3,32,128]{3,2,1,0:T(8,128)(2,1)}), bf16[16,3,32,128]{3,2,1,0:T(8,128)(2,1)S(1)}, u32[]{:S(2)}, u32[]{:S(2)}) async-start(bf16[16,3,32,128]{3,2,1,0:T(8,128)(2,1)} %shard_map.56), calls=%async_computation | async-start | bytes 786432 | tf_op jit(solution)/shard_map/all_to_all | solution.py:314
  74.8 11.7 %all-to-all-done = bf16[16,3,32,128]{3,2,1,0:T(8,128)(2,1)S(1)} async-done(((bf16[16,3,32,128]{3,2,1,0:T(8,128)(2,1)}), bf16[16,3,32,128]{3,2,1,0:T(8,128)(2,1)S(1)}, u32[]{:S(2)}, u32[]{:S(2)}) %all-to-all-start) | async-done | bytes 393248 | tf_op jit(solution)/shard_map/all_to_all | solution.py:314
  86.6 0.1 convert_reduce_fusion
  86.6 0.8 fusion.5
  87.4 0.6 pad_maximum_fusion.3
  (3 shorter events, 0.1 us)
Async XLA Ops:
  2.3 4.3 %copy-start.2 = (bf16[1,9,16,32,128]{4,3,2,1,0:T(8,128)(2,1)S(1)}, bf16[1,9,16,32,128]{4,3,2,1,0:T(8,128)(2,1)}, u32[]{:S(2)}) copy-start(bf16[1,9,16,32,128]{4,3,2,1,0:T(8,128)(2,1)} %param.5) | copy-start | bytes 3538948
  2.5 18.1 %collective-permute-start = (bf16[12,16,8,128]{3,2,1,0:T(8,128)(2,1)S(1)}, bf16[12,16,8,128]{3,2,1,0:T(8,128)(2,1)S(1)}, u32[]{:S(2)}, u32[]{:S(2)}) collective-permute-start(bf16[12,16,8,128]{3,2,1,0:T(8,128)(2,1)S(1)} %pad_maximum_fusion.1), channel_id=1, source_target_pairs={{0,1},{1,2},{2,3},{3,4},{4,5},{5,6},{6,7},{7,8},{8,9},{9,10},{10,1... | collective-permute-start | bytes 1179656 | tf_op jit(solution)/shard_map/ppermute | solution.py:310
  2.6 18.0 %collective-permute-start.1 = (bf16[12,16,8,128]{3,2,1,0:T(8,128)(2,1)S(1)}, bf16[12,16,8,128]{3,2,1,0:T(8,128)(2,1)S(1)}, u32[]{:S(2)}, u32[]{:S(2)}) collective-permute-start(bf16[12,16,8,128]{3,2,1,0:T(8,128)(2,1)S(1)} %pad_maximum_fusion.2), channel_id=1, source_target_pairs={{1,0},{2,1},{3,2},{4,3},{5,4},{6,5},{7,6},{8,7},{9,8},{10,9},{11,1... | collective-permute-start | bytes 1179656 | tf_op jit(solution)/shard_map/ppermute | solution.py:311
  6.6 3.7 %copy-start = (bf16[1,8,9,16,32,128]{5,4,3,2,1,0:T(8,128)(2,1)S(1)}, bf16[1,8,9,16,32,128]{5,4,3,2,1,0:T(8,128)(2,1)}, u32[]{:S(2)}) copy-start(bf16[1,8,9,16,32,128]{5,4,3,2,1,0:T(8,128)(2,1)} %forward.3) | copy-start | bytes 28311556
  10.3 10.3 %copy-start.1 = (bf16[1,8,9,16,32,128]{5,4,3,2,1,0:T(8,128)(2,1)S(1)}, bf16[1,8,9,16,32,128]{5,4,3,2,1,0:T(8,128)(2,1)}, u32[]{:S(2)}) copy-start(bf16[1,8,9,16,32,128]{5,4,3,2,1,0:T(8,128)(2,1)} %forward.3) | copy-start | bytes 28311556
  63.8 22.8 %all-to-all-start = ((bf16[16,3,32,128]{3,2,1,0:T(8,128)(2,1)}), bf16[16,3,32,128]{3,2,1,0:T(8,128)(2,1)S(1)}, u32[]{:S(2)}, u32[]{:S(2)}) async-start(bf16[16,3,32,128]{3,2,1,0:T(8,128)(2,1)} %shard_map.56), calls=%async_computation | async-start | bytes 786432 | tf_op jit(solution)/shard_map/all_to_all | solution.py:314

commit v2 on v1

--- a/solution.py
+++ b/solution.py
@@ -10,6 +10,7 @@
 F32, BF16 = jnp.float32, jnp.bfloat16
 HALO = 8
 PAD = 8
+FRONT = 8
 VX, VY, VZ, XX, YY, ZZ, XY, XZ, YZ = range(9)
 LAME, SHEAR2, BUOY = range(3)
 
@@ -158,11 +159,10 @@
 
         def load(level, carry):
             for field in range(9):
-                halo = left[field, level].astype(F32)
-                state[0, field, level + 1, pl.ds(8, 16)] = stair[0, field, level]
-                state[0, field, level + 1, pl.ds(0, 8)] = halo
-                state[1, field, level + 1, pl.ds(0, 16)] = stair[1, field, level]
-                state[1, field, level + 1, pl.ds(16, 8)] = right[field, level].astype(F32)
+                state[0, field, level + 1, pl.ds(FRONT, 8)] = left[field, level].astype(F32)
+                state[0, field, level + 1, pl.ds(FRONT + 8, 8)] = stair[0, field, level, pl.ds(0, 8)]
+                state[1, field, level + 1, pl.ds(0, 8)] = stair[1, field, level, pl.ds(8, 8)]
+                state[1, field, level + 1, pl.ds(FRONT, 8)] = right[field, level].astype(F32)
                 wide_f[0, field, level, pl.ds(0, 8)] = jnp.zeros((8, 128), F32)
                 wide_f[1, field, level, pl.ds(8, 8)] = jnp.zeros((8, 128), F32)
             for which in range(3):
@@ -170,47 +170,60 @@
                 mat[0, which, level, pl.ds(8, 16)] = coef[which, level, pl.ds(0, 16)]
                 mat[1, which, level, pl.ds(0, 16)] = coef[which, level, pl.ds(width - 16, 16)]
                 mat[1, which, level, pl.ds(16, 8)] = right[9 + which, level].astype(F32)
-                sums[which, level, pl.ds(0, 8)] = jnp.zeros((8, 128), F32)
-                sums[which, level, pl.ds(8, width)] = first_sums[which, level]
-                sums[which, level, pl.ds(8 + width, 8)] = jnp.zeros((8, 128), F32)
+                for side in range(2):
+                    sums[side, which, level] = jnp.zeros((24, 128), F32)
             return carry
 
         lax.fori_loop(0, levels, load, 0)
 
-    places = ((step, step + 1, step + 1), (15 - step, 15 - step, 39 - step))
-
-    def view(side, level, start):
-        def at(field, lev, lon):
-            return state[side, field, level + 1 + lev, pl.ds(start + lon, 8)]
-
-        def put(field, lon, value):
-            state[side, field, level + 1, pl.ds(start + lon, 8)] = value
-
-        return at, put
+    def widen(level):
+        for field in range(9):
+            wide_f[0, field, level, pl.ds(8, 8)] = forward[0, 0, field, level, pl.ds(0, 16)].astype(F32)[:8]
+            wide_f[1, field, level, pl.ds(0, 8)] = forward[0, 0, field, level, pl.ds(width - 16, 16)].astype(F32)[8:]
+
+    for level in range(levels):
+        widen(level)
+
+    old_x, new_x, old_s = (0, -1), (-1, 0), (1, -1)
+    x_coef, s_coef, f_row = (step, 15 - step), (step + 1, 15 - step), (step + 1, 7 - step)
 
     def velocity(level):
         for side in range(2):
-            start = places[side][0]
-            x_buoy = mat[side, BUOY, level, pl.ds(start, 8)]
-            yz_buoy = mat[side, BUOY, level, pl.ds(start + 1, 8)]
-            push(*view(side, level, start), (x_buoy, 1, yz_buoy))
+
+            def at(field, lev, lon):
+                return state[side, field, level + 1 + lev, pl.ds(FRONT + old_x[side] + lon, 8)]
+
+            def put(field, lon, value):
+                state[side, field, level + 1, pl.ds(FRONT + new_x[side] + lon, 8)] = value
+
+            x_buoy = mat[side, BUOY, level, pl.ds(x_coef[side], 8)]
+            yz_buoy = mat[side, BUOY, level, pl.ds(x_coef[side] + 1, 8)]
+            push(at, put, (x_buoy, 1, yz_buoy))
+        for field in (VX, VY, VZ):
+            first, row = (step, 7) if field == VX else (step + 1, 8)
+            state[0, field, level + 1, pl.ds(FRONT + row, 1)] = stair[0, field, level, pl.ds(first, 1)]
+            last, row = (14 - step, -1) if field == VX else (15 - step, 0)
+            state[1, field, level + 1, pl.ds(FRONT + row, 1)] = stair[1, field, level, pl.ds(last, 1)]
 
     def stress(level):
         for side in range(2):
-            _, start, place = places[side]
-            rows = pl.ds(start, 8)
-            parts = strain(*view(side, level, start), mat[side, LAME, level, rows], mat[side, SHEAR2, level, rows])
-            own = pl.ds(0, 16) if side == 0 else pl.ds(width - 16, 16)
-            for field in range(9):
-                value = forward[0, 0, field, level, own].astype(F32)
-                if side == 0:
-                    wide_f[side, field, level, pl.ds(8, 8)] = value[:8]
-                else:
-                    wide_f[side, field, level, pl.ds(0, 8)] = value[8:]
-            where_f = step + 1 if side == 0 else 7 - step
-            f = [wide_f[side, field, level, pl.ds(where_f, 8)] for field in range(9)]
+
+            def at(field, lev, lon):
+                row = FRONT + lon + (old_s[side] if field >= 3 else 0)
+                return state[side, field, level + 1 + lev, pl.ds(row, 8)]
+
+            def put(field, lon, value):
+                state[side, field, level + 1, pl.ds(FRONT + lon, 8)] = value
+
+            rows = pl.ds(s_coef[side], 8)
+            parts = strain(at, put, mat[side, LAME, level, rows], mat[side, SHEAR2, level, rows])
+            f = [wide_f[side, field, level, pl.ds(f_row[side], 8)] for field in range(9)]
             for which, term in enumerate(terms(*parts, f)):
-                sums[which, level, pl.ds(place, 8)] += term
+                before = sums[side, which, level, pl.ds(8 + old_s[side], 8)]
+                sums[side, which, level, pl.ds(8, 8)] = before + term
+        for field in range(3, 9):
+            state[0, field, level + 1, pl.ds(FRONT + 8, 1)] = stair[0, field, level, pl.ds(step + 1, 1)]
+            state[1, field, level + 1, pl.ds(FRONT - 1, 1)] = stair[1, field, level, pl.ds(14 - step, 1)]
 
     velocity(0)
     for level in range(levels):
@@ -222,7 +235,10 @@
     def _():
         def store(level, carry):
             for which, factor in enumerate((1.0, 2.0, 1.0)):
-                out[level, which] = (factor * sums[which, level, pl.ds(8, width)]).astype(BF16)
+                total = first_sums[which, level]
+                ends = [sums[side, which, level, pl.ds(8, 8)] for side in range(2)]
+                total = jnp.concatenate([total[:8] + ends[0], total[8:-8], total[-8:] + ends[1]])
+                out[level, which] = (factor * total).astype(BF16)
             return carry
 
         lax.fori_loop(0, levels, store, 0)
@@ -273,7 +289,7 @@
         scratch_shapes=[
             pltpu.VMEM((2, 9, levels + 2, 24, lat), F32),
             pltpu.VMEM((2, 3, levels, 24, lat), F32),
-            pltpu.VMEM((3, levels, width + 16, lat), F32),
+            pltpu.VMEM((2, 3, levels, 24, lat), F32),
             pltpu.VMEM((2, 9, levels, 16, lat), F32),
         ],
         compiler_params=pltpu.CompilerParams(vmem_limit_bytes=40 * 1024 * 1024),

time: 88.5 us -> 52.6 us (0.59)
  Pallas kernels: 53.5 us -> 17.6 us
    pallas_call x1, Pallas kernels: 43.2 us -> 7.33 us  [run_outer(): pl.pallas_call(functools.partial(outer, steps, levels, width), grid=(step...]
  transfers between devices with their start and end apart: 3 -> 3, of which waited for: 1 -> 1; matrix products, arithmetic and copies ran while one was open for 0% -> 0% of each run, Pallas kernels for 12% -> 20%
where the time goes in v2:
time: 52.6 us; the launch traced here: 52.2 us
  Pallas kernels  17.6 us (33%)
  starting transfers between devices  15 us (29%)
  waiting for transfers between devices  11.7 us (22%)
  local copies, waits for them, and re-layouts  4.82 us (9%)
  other arithmetic  2.86 us (5%)
    all_to_all x1, waiting for transfers between devices, shards(): parts = lax.all_to_all(partial, 'event', 0, 0, tiled=True)  11.7 us
    all_to_all x1, starting transfers between devices, shards(): parts = lax.all_to_all(partial, 'event', 0, 0, tiled=True)  11 us
    pallas_call x1, Pallas kernels, run_inner(): pl.pallas_call(functools.partial(inner, steps, levels, width), grid=(step...  10.3 us
    pallas_call x1, Pallas kernels, run_outer(): pl.pallas_call(functools.partial(outer, steps, levels, width), grid=(step...  7.33 us
    ppermute x1, starting transfers between devices, shards(): right = lax.ppermute(edge(0), 'lon', [(j, i) for i, j in up])  3.91 us
    unnamed x6, local copies, waits for them, and re-layouts  3.69 us
    another operation x2, other arithmetic, combine_kernels(): jnp.stack([2.0 * density * p_speed * p_speed * total[0], 2.0 * density *...  1.4 us
    another operation x2, other arithmetic, shards(): coef = jnp.stack([lame, shear2, 1.0 / density])  1.27 us
  transfers between devices with their start and end apart: 3, of which 1 were waited for; matrix products, arithmetic and copies ran while one was open for 0% of the time, Pallas kernels for 20%

profile of v2, /device:TPU:32, one launch (start us, length us, event | category | flops | bytes accessed | tf_op | source)
XLA Modules:
  0.0 52.2 jit_solution(3909713841148663006)
XLA Ops:
  0.0 1.1 %fusion.16 = (bf16[9,16,8,128]{3,2,1,0:T(8,128)(2,1)S(1)}, bf16[9,16,8,128]{3,2,1,0:T(8,128)(2,1)S(1)}) fusion(bf16[9,16,32,128]{3,2,1,0:T(8,128)(2,1)} %bitcast.13), kind=kLoop, calls=%fused_computation.29 | loop fusion | bytes 1179648 | tf_op jit(solution)/shard_map/slice | solution.py:321
  1.1 1.2 %fusion.2 = (f32[1,16,32,128]{3,2,1,0:T(8,128)S(1)}, f32[1,16,32,128]{3,2,1,0:T(8,128)S(1)}, f32[1,16,32,128]{3,2,1,0:T(8,128)S(1)}) fusion(f32[16,32,128]{2,1,0:T(8,128)} %param.9, f32[16,32,128]{2,1,0:T(8,128)} %param.8, f32[16,32,128]{2,1,0:T(8,128)} %param.7), kind=kLoop, calls=%fused_computation.8 | loop fusion | flops 589824 | bytes 1572864 | tf_op jit(solution)/shard_map/stack | solution.py:317
  2.3 0.0 copy-start.2
  2.4 0.1 fusion.15
  2.5 0.1 collective-permute-start
  2.6 3.9 %collective-permute-start.1 = (bf16[12,16,8,128]{3,2,1,0:T(8,128)(2,1)S(1)}, bf16[12,16,8,128]{3,2,1,0:T(8,128)(2,1)S(1)}, u32[]{:S(2)}, u32[]{:S(2)}) collective-permute-start(bf16[12,16,8,128]{3,2,1,0:T(8,128)(2,1)S(1)} %pad_maximum_fusion.2), channel_id=1, source_target_pairs={{1,0},{2,1},{3,2},{4,3},{5,4},{6,5},{7,6},{8,7},{9,8},{10,9},{11,1... | collective-permute-start | bytes 1179656 | tf_op jit(solution)/shard_map/ppermute | solution.py:327
  6.5 0.1 pad_maximum_fusion.coef
  6.6 0.0 copy-done.2
  6.6 0.0 copy-start
  6.6 3.7 %copy-done = bf16[1,8,9,16,32,128]{5,4,3,2,1,0:T(8,128)(2,1)S(1)} copy-done((bf16[1,8,9,16,32,128]{5,4,3,2,1,0:T(8,128)(2,1)S(1)}, bf16[1,8,9,16,32,128]{5,4,3,2,1,0:T(8,128)(2,1)}, u32[]{:S(2)}) %copy-start) | copy-done | bytes 9437208
  10.3 0.0 copy-start.1
  10.3 10.3 %shard_map.55 = (f32[3,16,32,128]{3,2,1,0:T(8,128)S(1)}, f32[2,9,16,16,128]{4,3,2,1,0:T(8,128)S(1)}) custom-call(bf16[9,16,32,128]{3,2,1,0:T(8,128)(2,1)S(1)} %bitcast.14, f32[3,16,32,128]{3,2,1,0:T(8,128)S(1)} %pad_maximum_fusion.coef, bf16[1,8,9,16,32,128]{5,4,3,2,1,0:T(8,128)(2,1)S(1)} %copy-done), custom_call_target="tpu_custom_call" | custom-call | flops 60000000 | bytes 30000000 | tf_op jit(solution)/shard_map/pallas_call | solution.py:257
  20.6 0.0 collective-permute-done.left
  20.6 0.0 collective-permute-done.1.right
  20.6 0.0 copy-done.1
  20.6 7.3 %shard_map.56 = bf16[16,3,32,128]{3,2,1,0:T(8,128)(2,1)} custom-call(bf16[12,16,8,128]{3,2,1,0:T(8,128)(2,1)S(1)} %collective-permute-done.left, bf16[12,16,8,128]{3,2,1,0:T(8,128)(2,1)S(1)} %collective-permute-done.1.right, f32[3,16,32,128]{3,2,1,0:T(8,128)S(1)} %pad_maximum_fusion.coef, bf16[1,8,9,16,32,128]{5,4,3,2,1,0:T(8,128)(2,1)S(1)} %copy-done.1, ...), custom_call_target="tpu_custom_call" | custom-call | flops 30000000 | bytes 20000000 | tf_op jit(solution)/shard_map/pallas_call | solution.py:276
  28.0 11.0 %all-to-all-start = ((bf16[16,3,32,128]{3,2,1,0:T(8,128)(2,1)}), bf16[16,3,32,128]{3,2,1,0:T(8,128)(2,1)S(1)}, u32[]{:S(2)}, u32[]{:S(2)}) async-start(bf16[16,3,32,128]{3,2,1,0:T(8,128)(2,1)} %shard_map.56), calls=%async_computation | async-start | bytes 786432 | tf_op jit(solution)/shard_map/all_to_all | solution.py:330
  39.0 11.7 %all-to-all-done = bf16[16,3,32,128]{3,2,1,0:T(8,128)(2,1)S(1)} async-done(((bf16[16,3,32,128]{3,2,1,0:T(8,128)(2,1)}), bf16[16,3,32,128]{3,2,1,0:T(8,128)(2,1)S(1)}, u32[]{:S(2)}, u32[]{:S(2)}) %all-to-all-start) | async-done | bytes 393248 | tf_op jit(solution)/shard_map/all_to_all | solution.py:330
  50.8 0.1 convert_reduce_fusion
  50.8 0.8 %fusion.5 = (f32[1,1,32,128]{3,2,1,0:T(8,128)S(1)}, f32[1,1,32,128]{3,2,1,0:T(8,128)S(1)}, f32[1,1,32,128]{3,2,1,0:T(8,128)S(1)}) fusion(f32[16,32,128]{2,1,0:T(8,128)} %param.7, s32[]{:T(128)S(6)} %select_n.2, f32[3,32,128]{2,1,0:T(8,128)S(1)} %convert_reduce_fusion, f32[16,32,128]{2,1,0:T(8,128)} %param.9, f32[16,32,128]{2,1,0:T(8,128)} %param.8), kind=kLoop, calls=%fused_computation.17 | loop fusion | flops 86016 | bytes 147460 | tf_op jit(solution)/shard_map/stack | solution.py:303
  51.6 0.6 %pad_maximum_fusion.3 = f32[3,1,32,128]{3,2,1,0:T(8,128)} fusion(f32[1,1,32,128]{3,2,1,0:T(8,128)S(1)} %get-tuple-element.12, f32[1,1,32,128]{3,2,1,0:T(8,128)S(1)} %get-tuple-element.13, f32[1,1,32,128]{3,2,1,0:T(8,128)S(1)} %get-tuple-element.11), kind=kLoop, calls=%fused_computation.11 | loop fusion | flops 24576 | bytes 98304 | tf_op jit(solution)/shard_map/stack | solution.py:303
  (3 shorter events, 0.1 us)
Async XLA Ops:
  2.3 4.3 %copy-start.2 = (bf16[1,9,16,32,128]{4,3,2,1,0:T(8,128)(2,1)S(1)}, bf16[1,9,16,32,128]{4,3,2,1,0:T(8,128)(2,1)}, u32[]{:S(2)}) copy-start(bf16[1,9,16,32,128]{4,3,2,1,0:T(8,128)(2,1)} %param.5) | copy-start | bytes 3538948
  2.5 18.1 %collective-permute-start = (bf16[12,16,8,128]{3,2,1,0:T(8,128)(2,1)S(1)}, bf16[12,16,8,128]{3,2,1,0:T(8,128)(2,1)S(1)}, u32[]{:S(2)}, u32[]{:S(2)}) collective-permute-start(bf16[12,16,8,128]{3,2,1,0:T(8,128)(2,1)S(1)} %pad_maximum_fusion.1), channel_id=1, source_target_pairs={{0,1},{1,2},{2,3},{3,4},{4,5},{5,6},{6,7},{7,8},{8,9},{9,10},{10,1... | collective-permute-start | bytes 1179656 | tf_op jit(solution)/shard_map/ppermute | solution.py:326
  2.6 18.0 %collective-permute-start.1 = (bf16[12,16,8,128]{3,2,1,0:T(8,128)(2,1)S(1)}, bf16[12,16,8,128]{3,2,1,0:T(8,128)(2,1)S(1)}, u32[]{:S(2)}, u32[]{:S(2)}) collective-permute-start(bf16[12,16,8,128]{3,2,1,0:T(8,128)(2,1)S(1)} %pad_maximum_fusion.2), channel_id=1, source_target_pairs={{1,0},{2,1},{3,2},{4,3},{5,4},{6,5},{7,6},{8,7},{9,8},{10,9},{11,1... | collective-permute-start | bytes 1179656 | tf_op jit(solution)/shard_map/ppermute | solution.py:327
  6.6 3.7 %copy-start = (bf16[1,8,9,16,32,128]{5,4,3,2,1,0:T(8,128)(2,1)S(1)}, bf16[1,8,9,16,32,128]{5,4,3,2,1,0:T(8,128)(2,1)}, u32[]{:S(2)}) copy-start(bf16[1,8,9,16,32,128]{5,4,3,2,1,0:T(8,128)(2,1)} %forward.3) | copy-start | bytes 28311556
  10.3 10.3 %copy-start.1 = (bf16[1,8,9,16,32,128]{5,4,3,2,1,0:T(8,128)(2,1)S(1)}, bf16[1,8,9,16,32,128]{5,4,3,2,1,0:T(8,128)(2,1)}, u32[]{:S(2)}) copy-start(bf16[1,8,9,16,32,128]{5,4,3,2,1,0:T(8,128)(2,1)} %forward.3) | copy-start | bytes 28311556
  28.0 22.8 %all-to-all-start = ((bf16[16,3,32,128]{3,2,1,0:T(8,128)(2,1)}), bf16[16,3,32,128]{3,2,1,0:T(8,128)(2,1)S(1)}, u32[]{:S(2)}, u32[]{:S(2)}) async-start(bf16[16,3,32,128]{3,2,1,0:T(8,128)(2,1)} %shard_map.56), calls=%async_computation | async-start | bytes 786432 | tf_op jit(solution)/shard_map/all_to_all | solution.py:330

commit v3 on v2

--- a/solution.py
+++ b/solution.py
@@ -244,8 +244,70 @@
         lax.fori_loop(0, levels, store, 0)
 
 
-def whole(array):
-    return pl.BlockSpec(array.shape, lambda t, n=len(array.shape): (0,) * n)
+def prepare(levels, width, row, init, p_speed, s_speed, density, first, last, coef, own):
+    def load(level, carry):
+        rho, p, s = density[level], p_speed[level], s_speed[level]
+        parts = (rho * (p * p - 2.0 * s * s), 2.0 * rho * s * s, 1.0 / rho)
+        for which, part in enumerate(parts):
+            coef[which, level] = part
+            first[9 + which, level] = part[:HALO].astype(BF16)
+            last[9 + which, level] = part[width - HALO :].astype(BF16)
+        for field in range(9):
+            first[field, level] = init[field, level, pl.ds(0, 16)].astype(F32)[:HALO].astype(BF16)
+            last[field, level] = init[field, level, pl.ds(width - 16, 16)].astype(F32)[16 - HALO :].astype(BF16)
+        return carry
+
+    lax.fori_loop(0, levels, load, 0, unroll=4)
+    for which, item in enumerate((p_speed, s_speed, density)):
+        own[which] = item[row[0]]
+
+
+def finish(events, parts, own, out):
+    total = [parts[0, which].astype(F32) for which in range(3)]
+    for event in range(1, events):
+        total = [so_far + parts[event, which].astype(F32) for which, so_far in enumerate(total)]
+    p_speed, s_speed, density = own[0], own[1], own[2]
+    lame = density * (p_speed * p_speed - 2.0 * s_speed * s_speed)
+    shear = density * s_speed * s_speed
+    out[0, 0] = 2.0 * density * p_speed * p_speed * total[0]
+    out[1, 0] = 2.0 * density * s_speed * s_speed * (total[1] - 2.0 * total[0])
+    out[2, 0] = density * total[2] + lame * total[0] + shear * total[1]
+
+
+IN_VMEM = pl.BlockSpec(memory_space=pltpu.VMEM)
+MEBI = 1024 * 1024
+
+
+def run_prepare(row, init, p_speed, s_speed, density):
+    _, levels, width, lat = init.shape
+    edge = jax.ShapeDtypeStruct((12, levels, HALO, lat), BF16)
+    return pl.pallas_call(
+        functools.partial(prepare, levels, width),
+        in_specs=[pl.BlockSpec(memory_space=pltpu.SMEM)] + [IN_VMEM] * 4,
+        out_specs=[IN_VMEM] * 4,
+        out_shape=[
+            edge,
+            edge,
+            jax.ShapeDtypeStruct((3, levels, width, lat), F32),
+            jax.ShapeDtypeStruct((3, width, lat), F32),
+        ],
+        compiler_params=pltpu.CompilerParams(vmem_limit_bytes=16 * MEBI),
+    )(row, init, p_speed, s_speed, density)
+
+
+def run_finish(parts, own):
+    events, _, width, lat = parts.shape
+    return pl.pallas_call(
+        functools.partial(finish, events),
+        in_specs=[IN_VMEM] * 2,
+        out_specs=IN_VMEM,
+        out_shape=jax.ShapeDtypeStruct((3, 1, width, lat), F32),
+        compiler_params=pltpu.CompilerParams(vmem_limit_bytes=8 * MEBI),
+    )(parts, own)
+
+
+def by_step(forward):
+    return pl.BlockSpec((1, 1) + forward.shape[2:], lambda t: (0, t, 0, 0, 0, 0))
 
 
 def run_inner(init, coef, forward):
@@ -257,81 +319,46 @@
     return pl.pallas_call(
         functools.partial(inner, steps, levels, width),
         grid=(steps,),
-        in_specs=[
-            whole(init),
-            whole(coef),
-            pl.BlockSpec((1, 1, 9, levels, width, lat), lambda t: (0, t, 0, 0, 0, 0)),
-        ],
-        out_specs=[whole(item) for item in outs],
+        in_specs=[IN_VMEM, IN_VMEM, by_step(forward)],
+        out_specs=[IN_VMEM] * 2,
         out_shape=outs,
         scratch_shapes=[pltpu.VMEM((9, levels + 2, width + 2 * PAD, lat), F32)],
-        compiler_params=pltpu.CompilerParams(vmem_limit_bytes=30 * 1024 * 1024),
+        compiler_params=pltpu.CompilerParams(vmem_limit_bytes=46 * MEBI),
         cost_estimate=pl.CostEstimate(flops=60_000_000, bytes_accessed=30_000_000, transcendentals=0),
     )(init, coef, forward)
 
 
 def run_outer(left, right, coef, forward, first_sums, stair):
     _, steps, _, levels, width, lat = forward.shape
-    out = jax.ShapeDtypeStruct((levels, 3, width, lat), BF16)
     return pl.pallas_call(
         functools.partial(outer, steps, levels, width),
         grid=(steps,),
-        in_specs=[
-            whole(left),
-            whole(right),
-            whole(coef),
-            pl.BlockSpec((1, 1, 9, levels, width, lat), lambda t: (0, t, 0, 0, 0, 0)),
-            whole(first_sums),
-            whole(stair),
-        ],
-        out_specs=whole(out),
-        out_shape=out,
+        in_specs=[IN_VMEM] * 3 + [by_step(forward)] + [IN_VMEM] * 2,
+        out_specs=IN_VMEM,
+        out_shape=jax.ShapeDtypeStruct((levels, 3, width, lat), BF16),
         scratch_shapes=[
             pltpu.VMEM((2, 9, levels + 2, 24, lat), F32),
             pltpu.VMEM((2, 3, levels, 24, lat), F32),
             pltpu.VMEM((2, 3, levels, 24, lat), F32),
             pltpu.VMEM((2, 9, levels, 16, lat), F32),
         ],
-        compiler_params=pltpu.CompilerParams(vmem_limit_bytes=40 * 1024 * 1024),
+        compiler_params=pltpu.CompilerParams(vmem_limit_bytes=46 * MEBI),
         cost_estimate=pl.CostEstimate(flops=30_000_000, bytes_accessed=20_000_000, transcendentals=0),
     )(left, right, coef, forward, first_sums, stair)
 
 
-def combine_kernels(total, p_speed, s_speed, density):
-    lame = density * (p_speed * p_speed - 2.0 * s_speed * s_speed)
-    shear = density * s_speed * s_speed
-    return jnp.stack(
-        [
-            2.0 * density * p_speed * p_speed * total[0],
-            2.0 * density * s_speed * s_speed * (total[1] - 2.0 * total[0]),
-            density * total[2] + lame * total[0] + shear * total[1],
-        ]
-    )
-
-
 def shards(adjoint_init, forward_state, p_speed, s_speed, density):
     init = adjoint_init[0]
-    width = init.shape[2]
-    lame = density * (p_speed * p_speed - 2.0 * s_speed * s_speed)
-    shear2 = 2.0 * density * s_speed * s_speed
-    coef = jnp.stack([lame, shear2, 1.0 / density])
-
-    def edge(start):
-        return jnp.concatenate(
-            [init[:, :, start : start + HALO], coef[:, :, start : start + HALO].astype(BF16)]
-        )
-
+    row = lax.axis_index("event").reshape(1)
+    first, last, coef, own = run_prepare(row, init, p_speed, s_speed, density)
     count = lax.axis_size("lon")
     up = [(i, (i + 1) % count) for i in range(count)]
-    left = lax.ppermute(edge(width - HALO), "lon", up)
-    right = lax.ppermute(edge(0), "lon", [(j, i) for i, j in up])
+    left = lax.ppermute(last, "lon", up)
+    right = lax.ppermute(first, "lon", [(j, i) for i, j in up])
     first_sums, stair = run_inner(init, coef, forward_state)
     partial = run_outer(left, right, coef, forward_state, first_sums, stair)
     parts = lax.all_to_all(partial, "event", 0, 0, tiled=True)
-    total = jnp.sum(parts.astype(F32), axis=0, keepdims=False)[:, None]
-    first_row = lax.axis_index("event")
-    own = [lax.dynamic_slice_in_dim(item, first_row, 1, 0) for item in (p_speed, s_speed, density)]
-    return combine_kernels(total, *own)
+    return run_finish(parts, own)
 
 
 def solution(mesh):

time: 52.6 us -> 53.7 us (1.021)
  blocking collectives: 0 us -> 22.6 us
  waiting for transfers between devices: 11.7 us -> 0.01 us
  starting transfers between devices: 15 us -> 3.93 us
  Pallas kernels: 17.6 us -> 22.4 us
  other arithmetic: 2.86 us -> 0 us
  local copies, waits for them, and re-layouts: 4.82 us -> 4.12 us
    all_to_all x0 -> x1, blocking collectives: none -> 22.6 us  [shards(): parts = lax.all_to_all(partial, 'event', 0, 0, tiled=True)]
    all_to_all x1 -> x0, waiting for transfers between devices: 11.7 us -> none  [shards(): parts = lax.all_to_all(partial, 'event', 0, 0, tiled=True)]
    all_to_all x1 -> x0, starting transfers between devices: 11 us -> none  [shards(): parts = lax.all_to_all(partial, 'event', 0, 0, tiled=True)]
    another operation x5 -> x0, other arithmetic: 2.73 us -> none  [the longest x2 1.4 us: combine_kernels(): jnp.stack([2.0 * density * p_speed * p_speed * total[0], 2.0 * density *...]
    pallas_call x1, Pallas kernels: 7.33 us -> 9.68 us  [run_outer(): pl.pallas_call(functools.partial(outer, steps, levels, width), grid=(step...]
    pallas_call x1, Pallas kernels: 10.3 us -> 11.8 us  [run_inner(): pl.pallas_call(functools.partial(inner, steps, levels, width), grid=(step...]
    slice x2 -> x0, local copies, waits for them, and re-layouts: 1.14 us -> none  [the longest x1 1.1 us: edge(): init[:, :, start:start + HALO]]
    pallas_call x0 -> x2, Pallas kernels: none -> 0.94 us  [the longest x1 0.69 us: run_finish(): pl.pallas_call(functools.partial(finish, events), in_specs=[IN_VMEM] * 2,...]
  transfers between devices with their start and end apart: 3 -> 2, of which waited for: 1 -> 0; matrix products, arithmetic and copies ran while one was open for 0% -> 0% of each run, Pallas kernels for 20% -> 22%
where the time goes in v3:
time: 53.7 us; the launch traced here: 53.1 us
  blocking collectives  22.6 us (42%)
  Pallas kernels  22.4 us (42%)
  local copies, waits for them, and re-layouts  4.12 us (8%)
  starting transfers between devices  3.93 us (7%)
    all_to_all x1, blocking collectives, shards(): parts = lax.all_to_all(partial, 'event', 0, 0, tiled=True)  22.6 us
    pallas_call x1, Pallas kernels, run_inner(): pl.pallas_call(functools.partial(inner, steps, levels, width), grid=(step...  11.8 us
    pallas_call x1, Pallas kernels, run_outer(): pl.pallas_call(functools.partial(outer, steps, levels, width), grid=(step...  9.68 us
    unnamed x10, local copies, waits for them, and re-layouts  4.12 us
    ppermute x1, starting transfers between devices, shards(): right = lax.ppermute(first, 'lon', [(j, i) for i, j in up])  3.84 us
  transfers between devices with their start and end apart: 2, of which 0 were waited for; matrix products, arithmetic and copies ran while one was open for 0% of the time, Pallas kernels for 22%

profile of v3, /device:TPU:32, one launch (start us, length us, event | category | flops | bytes accessed | tf_op | source)
XLA Modules:
  0.0 53.1 jit_solution(6064852146755983122)
XLA Ops:
  0.0 0.0 copy-start
  0.0 1.3 %copy-done = bf16[1,9,16,32,128]{4,3,2,1,0:T(8,128)(2,1)S(1)} copy-done((bf16[1,9,16,32,128]{4,3,2,1,0:T(8,128)(2,1)S(1)}, bf16[1,9,16,32,128]{4,3,2,1,0:T(8,128)(2,1)}, u32[]{:S(2)}) %copy-start) | copy-done | bytes 1179672
  1.3 0.0 copy-start.2
  1.3 0.9 %copy-done.2 = f32[16,32,128]{2,1,0:T(8,128)S(1)} copy-done((f32[16,32,128]{2,1,0:T(8,128)S(1)}, f32[16,32,128]{2,1,0:T(8,128)}, u32[]{:S(2)}) %copy-start.2) | copy-done | bytes 262168
  2.2 0.0 copy-start.3
  2.2 0.9 %copy-done.3 = f32[16,32,128]{2,1,0:T(8,128)S(1)} copy-done((f32[16,32,128]{2,1,0:T(8,128)S(1)}, f32[16,32,128]{2,1,0:T(8,128)}, u32[]{:S(2)}) %copy-start.3) | copy-done | bytes 262168
  3.2 0.0 copy-start.4
  3.2 0.9 %copy-done.4 = f32[16,32,128]{2,1,0:T(8,128)S(1)} copy-done((f32[16,32,128]{2,1,0:T(8,128)S(1)}, f32[16,32,128]{2,1,0:T(8,128)}, u32[]{:S(2)}) %copy-start.4) | copy-done | bytes 262168
  4.1 0.0 copy-start.1
  4.1 0.2 shard_map.55
  4.4 0.1 collective-permute-start
  4.5 3.8 %collective-permute-start.1 = (bf16[12,16,8,128]{3,2,1,0:T(8,128)(2,1)S(1)}, bf16[12,16,8,128]{3,2,1,0:T(8,128)(2,1)S(1)}, u32[]{:S(2)}, u32[]{:S(2)}) collective-permute-start(bf16[12,16,8,128]{3,2,1,0:T(8,128)(2,1)S(1)} %get-tuple-element.12), channel_id=1, source_target_pairs={{1,0},{2,1},{3,2},{4,3},{5,4},{6,5},{7,6},{8,7},{9,8},{10,9},{11,1... | collective-permute-start | bytes 1179656 | tf_op jit(solution)/shard_map/ppermute | solution.py:357
  8.3 0.0 copy-done.1
  8.3 11.8 %shard_map.56 = (f32[3,16,32,128]{3,2,1,0:T(8,128)S(1)}, f32[2,9,16,16,128]{4,3,2,1,0:T(8,128)S(1)}) custom-call(bf16[9,16,32,128]{3,2,1,0:T(8,128)(2,1)S(1)} %bitcast.3, f32[3,16,32,128]{3,2,1,0:T(8,128)S(1)} %get-tuple-element.13.coef, bf16[1,8,9,16,32,128]{5,4,3,2,1,0:T(8,128)(2,1)} %forward.3), custom_call_target="tpu_custom_call" | custom-call | flops 60000000 | bytes 30000000 | tf_op jit(solution)/shard_map/pallas_call | solution.py:319
  20.1 0.0 collective-permute-done.left
  20.1 0.0 collective-permute-done.1.right
  20.1 9.7 %shard_map.57 = bf16[16,3,32,128]{3,2,1,0:T(8,128)(2,1)S(1)} custom-call(bf16[12,16,8,128]{3,2,1,0:T(8,128)(2,1)S(1)} %collective-permute-done.left, bf16[12,16,8,128]{3,2,1,0:T(8,128)(2,1)S(1)} %collective-permute-done.1.right, f32[3,16,32,128]{3,2,1,0:T(8,128)S(1)} %get-tuple-element.13.coef, bf16[1,8,9,16,32,128]{5,4,3,2,1,0:T(8,128)(2,1)} %forward.3, ...), custom_call_target="tpu_custom_call" | custom-call | flops 30000000 | bytes 20000000 | tf_op jit(solution)/shard_map/pallas_call | solution.py:333
  29.8 22.6 %all_to_all.5.parts = bf16[16,3,32,128]{3,2,1,0:T(8,128)(2,1)S(1)} all-to-all(bf16[16,3,32,128]{3,2,1,0:T(8,128)(2,1)S(1)} %shard_map.57), channel_id=1, replica_groups=mesh['event'=16,'lon'=16] {'event'}, dimensions={0} | all-to-all | bytes 786432 | tf_op jit(solution)/shard_map/all_to_all | solution.py:360
  52.4 0.7 %shard_map.58 = f32[3,1,32,128]{3,2,1,0:T(8,128)} custom-call(bf16[16,3,32,128]{3,2,1,0:T(8,128)(2,1)S(1)} %all_to_all.5.parts, f32[3,32,128]{2,1,0:T(8,128)S(1)} %get-tuple-element.16.own), custom_call_target="tpu_custom_call" | custom-call | tf_op jit(solution)/shard_map/pallas_call | solution.py:300
Async XLA Ops:
  0.0 1.3 %copy-start = (bf16[1,9,16,32,128]{4,3,2,1,0:T(8,128)(2,1)S(1)}, bf16[1,9,16,32,128]{4,3,2,1,0:T(8,128)(2,1)}, u32[]{:S(2)}) copy-start(bf16[1,9,16,32,128]{4,3,2,1,0:T(8,128)(2,1)} %param.5) | copy-start | bytes 3538948
  1.3 0.9 %copy-start.2 = (f32[16,32,128]{2,1,0:T(8,128)S(1)}, f32[16,32,128]{2,1,0:T(8,128)}, u32[]{:S(2)}) copy-start(f32[16,32,128]{2,1,0:T(8,128)} %p_speed.1) | copy-start | bytes 786436
  2.2 0.9 %copy-start.3 = (f32[16,32,128]{2,1,0:T(8,128)S(1)}, f32[16,32,128]{2,1,0:T(8,128)}, u32[]{:S(2)}) copy-start(f32[16,32,128]{2,1,0:T(8,128)} %s_speed.1) | copy-start | bytes 786436
  3.2 0.9 %copy-start.4 = (f32[16,32,128]{2,1,0:T(8,128)S(1)}, f32[16,32,128]{2,1,0:T(8,128)}, u32[]{:S(2)}) copy-start(f32[16,32,128]{2,1,0:T(8,128)} %density.1) | copy-start | bytes 786436
  4.1 4.2 %copy-start.1 = (bf16[1,9,16,32,128]{4,3,2,1,0:T(8,128)(2,1)S(1)}, bf16[1,9,16,32,128]{4,3,2,1,0:T(8,128)(2,1)}, u32[]{:S(2)}) copy-start(bf16[1,9,16,32,128]{4,3,2,1,0:T(8,128)(2,1)} %param.5) | copy-start | bytes 3538948
  4.4 15.8 %collective-permute-start = (bf16[12,16,8,128]{3,2,1,0:T(8,128)(2,1)S(1)}, bf16[12,16,8,128]{3,2,1,0:T(8,128)(2,1)S(1)}, u32[]{:S(2)}, u32[]{:S(2)}) collective-permute-start(bf16[12,16,8,128]{3,2,1,0:T(8,128)(2,1)S(1)} %get-tuple-element.11), channel_id=1, source_target_pairs={{0,1},{1,2},{2,3},{3,4},{4,5},{5,6},{6,7},{7,8},{8,9},{9,10},{10,1... | collective-permute-start | bytes 1179656 | tf_op jit(solution)/shard_map/ppermute | solution.py:356
  4.5 15.7 %collective-permute-start.1 = (bf16[12,16,8,128]{3,2,1,0:T(8,128)(2,1)S(1)}, bf16[12,16,8,128]{3,2,1,0:T(8,128)(2,1)S(1)}, u32[]{:S(2)}, u32[]{:S(2)}) collective-permute-start(bf16[12,16,8,128]{3,2,1,0:T(8,128)(2,1)S(1)} %get-tuple-element.12), channel_id=1, source_target_pairs={{1,0},{2,1},{3,2},{4,3},{5,4},{6,5},{7,6},{8,7},{9,8},{10,9},{11,1... | collective-permute-start | bytes 1179656 | tf_op jit(solution)/shard_map/ppermute | solution.py:357

commit v4 on v3

--- a/solution.py
+++ b/solution.py
@@ -79,14 +79,19 @@
     )
 
 
-def inner(steps, levels, width, init, coef, forward, sums, stair, state):
+def inner(steps, levels, width, init, coef, forward_hbm, sums, stair, forward, state, arrived):
     step = pl.program_id(0)
+
+    def fetch(which):
+        return pltpu.make_async_copy(forward_hbm.at[0, which], forward.at[which], arrived.at[which])
 
     def keep(level, side, field, row, value):
         stair[side, field, level, pl.ds(row, 1)] = value
 
     @pl.when(step == 0)
     def _():
+        for which in range(steps):
+            fetch(which).start()
         empty = jnp.zeros((9, 1, width + 2 * PAD, 128), F32)
         state[:, pl.ds(0, 1)] = empty
         state[:, pl.ds(levels + 1, 1)] = empty
@@ -131,7 +136,7 @@
         for start in range(0, width, 16):
             mine = pl.ds(start, 16)
             parts = strain(*view(level, start, 16), coef[LAME, level, mine], coef[SHEAR2, level, mine])
-            f = [forward[0, 0, field, level, mine].astype(F32) for field in range(9)]
+            f = [forward[step, field, level, mine].astype(F32) for field in range(9)]
             column = start + lax.broadcasted_iota(jnp.int32, (16, 128), 0)
             right = (column > step) & (column < width - 1 - step)
             for which, term in enumerate(terms(*parts, f)):
@@ -140,6 +145,7 @@
             keep(level, 0, field, step + 1, state[field, level + 1, pl.ds(PAD + step + 1, 1)])
             keep(level, 1, field, 14 - step, state[field, level + 1, pl.ds(PAD + 30 - step, 1)])
 
+    fetch(step).wait()
     velocity(0)
     for level in range(levels):
         if level + 1 < levels:
@@ -178,8 +184,8 @@
 
     def widen(level):
         for field in range(9):
-            wide_f[0, field, level, pl.ds(8, 8)] = forward[0, 0, field, level, pl.ds(0, 16)].astype(F32)[:8]
-            wide_f[1, field, level, pl.ds(0, 8)] = forward[0, 0, field, level, pl.ds(width - 16, 16)].astype(F32)[8:]
+            wide_f[0, field, level, pl.ds(8, 8)] = forward[step, field, level, pl.ds(0, 16)].astype(F32)[:8]
+            wide_f[1, field, level, pl.ds(0, 8)] = forward[step, field, level, pl.ds(width - 16, 16)].astype(F32)[8:]
 
     for level in range(levels):
         widen(level)
@@ -244,9 +250,9 @@
         lax.fori_loop(0, levels, store, 0)
 
 
-def prepare(levels, width, row, init, p_speed, s_speed, density, first, last, coef, own):
+def prepare(levels, width, row, init, material, first, last, coef, own):
     def load(level, carry):
-        rho, p, s = density[level], p_speed[level], s_speed[level]
+        p, s, rho = [material[which, level] for which in range(3)]
         parts = (rho * (p * p - 2.0 * s * s), 2.0 * rho * s * s, 1.0 / rho)
         for which, part in enumerate(parts):
             coef[which, level] = part
@@ -258,8 +264,8 @@
         return carry
 
     lax.fori_loop(0, levels, load, 0, unroll=4)
-    for which, item in enumerate((p_speed, s_speed, density)):
-        own[which] = item[row[0]]
+    for which in range(3):
+        own[which] = material[which, row[0]]
 
 
 def finish(events, parts, own, out):
@@ -275,15 +281,16 @@
 
 
 IN_VMEM = pl.BlockSpec(memory_space=pltpu.VMEM)
+IN_HBM = pl.BlockSpec(memory_space=pltpu.HBM)
 MEBI = 1024 * 1024
 
 
-def run_prepare(row, init, p_speed, s_speed, density):
+def run_prepare(row, init, material):
     _, levels, width, lat = init.shape
     edge = jax.ShapeDtypeStruct((12, levels, HALO, lat), BF16)
     return pl.pallas_call(
         functools.partial(prepare, levels, width),
-        in_specs=[pl.BlockSpec(memory_space=pltpu.SMEM)] + [IN_VMEM] * 4,
+        in_specs=[pl.BlockSpec(memory_space=pltpu.SMEM)] + [IN_VMEM] * 2,
         out_specs=[IN_VMEM] * 4,
         out_shape=[
             edge,
@@ -292,7 +299,7 @@
             jax.ShapeDtypeStruct((3, width, lat), F32),
         ],
         compiler_params=pltpu.CompilerParams(vmem_limit_bytes=16 * MEBI),
-    )(row, init, p_speed, s_speed, density)
+    )(row, init, material)
 
 
 def run_finish(parts, own):
@@ -306,34 +313,34 @@
     )(parts, own)
 
 
-def by_step(forward):
-    return pl.BlockSpec((1, 1) + forward.shape[2:], lambda t: (0, t, 0, 0, 0, 0))
-
-
 def run_inner(init, coef, forward):
     _, steps, _, levels, width, lat = forward.shape
     outs = [
         jax.ShapeDtypeStruct((3, levels, width, lat), F32),
         jax.ShapeDtypeStruct((2, 9, levels, 16, lat), F32),
+        jax.ShapeDtypeStruct(forward.shape[1:], BF16),
     ]
     return pl.pallas_call(
         functools.partial(inner, steps, levels, width),
         grid=(steps,),
-        in_specs=[IN_VMEM, IN_VMEM, by_step(forward)],
-        out_specs=[IN_VMEM] * 2,
+        in_specs=[IN_VMEM, IN_VMEM, IN_HBM],
+        out_specs=[IN_VMEM] * 3,
         out_shape=outs,
-        scratch_shapes=[pltpu.VMEM((9, levels + 2, width + 2 * PAD, lat), F32)],
-        compiler_params=pltpu.CompilerParams(vmem_limit_bytes=46 * MEBI),
+        scratch_shapes=[
+            pltpu.VMEM((9, levels + 2, width + 2 * PAD, lat), F32),
+            pltpu.SemaphoreType.DMA((steps,)),
+        ],
+        compiler_params=pltpu.CompilerParams(vmem_limit_bytes=34 * MEBI),
         cost_estimate=pl.CostEstimate(flops=60_000_000, bytes_accessed=30_000_000, transcendentals=0),
     )(init, coef, forward)
 
 
 def run_outer(left, right, coef, forward, first_sums, stair):
-    _, steps, _, levels, width, lat = forward.shape
+    steps, _, levels, width, lat = forward.shape
     return pl.pallas_call(
         functools.partial(outer, steps, levels, width),
         grid=(steps,),
-        in_specs=[IN_VMEM] * 3 + [by_step(forward)] + [IN_VMEM] * 2,
+        in_specs=[IN_VMEM] * 6,
         out_specs=IN_VMEM,
         out_shape=jax.ShapeDtypeStruct((levels, 3, width, lat), BF16),
         scratch_shapes=[
@@ -342,7 +349,7 @@
             pltpu.VMEM((2, 3, levels, 24, lat), F32),
             pltpu.VMEM((2, 9, levels, 16, lat), F32),
         ],
-        compiler_params=pltpu.CompilerParams(vmem_limit_bytes=46 * MEBI),
+        compiler_params=pltpu.CompilerParams(vmem_limit_bytes=34 * MEBI),
         cost_estimate=pl.CostEstimate(flops=30_000_000, bytes_accessed=20_000_000, transcendentals=0),
     )(left, right, coef, forward, first_sums, stair)
 
@@ -350,13 +357,13 @@
 def shards(adjoint_init, forward_state, p_speed, s_speed, density):
     init = adjoint_init[0]
     row = lax.axis_index("event").reshape(1)
-    first, last, coef, own = run_prepare(row, init, p_speed, s_speed, density)
+    first, last, coef, own = run_prepare(row, init, jnp.stack([p_speed, s_speed, density]))
     count = lax.axis_size("lon")
     up = [(i, (i + 1) % count) for i in range(count)]
     left = lax.ppermute(last, "lon", up)
     right = lax.ppermute(first, "lon", [(j, i) for i, j in up])
-    first_sums, stair = run_inner(init, coef, forward_state)
-    partial = run_outer(left, right, coef, forward_state, first_sums, stair)
+    first_sums, stair, forward = run_inner(init, coef, forward_state)
+    partial = run_outer(left, right, coef, forward, first_sums, stair)
     parts = lax.all_to_all(partial, "event", 0, 0, tiled=True)
     return run_finish(parts, own)
 

time: 53.7 us -> 48.1 us (0.90)
  Pallas kernels: 22.4 us -> 17.5 us
  local copies, waits for them, and re-layouts: 4.12 us -> 2.54 us
  other arithmetic: 0 us -> 1.16 us
    pallas_call x1, Pallas kernels: 9.68 us -> 6.59 us  [run_outer(): pl.pallas_call(functools.partial(outer, steps, levels, width), grid=(step...]
    pallas_call x1, Pallas kernels: 11.8 us -> 10 us  [run_inner(): pl.pallas_call(functools.partial(inner, steps, levels, width), grid=(step...]
    unnamed x10 -> x4, local copies, waits for them, and re-layouts: 4.12 us -> 2.54 us
    another operation x0 -> x1, other arithmetic: none -> 1.16 us  [shards(): jnp.stack([p_speed, s_speed, density])]
  transfers between devices with their start and end apart: 2 -> 2, of which waited for: 0 -> 0; matrix products, arithmetic and copies ran while one was open for 0% -> 0% of each run, Pallas kernels for 22% -> 21%
where the time goes in v4:
time: 48.1 us; the launch traced here: 47.8 us
  blocking collectives  22.6 us (47%)
  Pallas kernels  17.5 us (36%)
  starting transfers between devices  3.93 us (8%)
  local copies, waits for them, and re-layouts  2.54 us (5%)
  other arithmetic  1.16 us (2%)
    all_to_all x1, blocking collectives, shards(): parts = lax.all_to_all(partial, 'event', 0, 0, tiled=True)  22.6 us
    pallas_call x1, Pallas kernels, run_inner(): pl.pallas_call(functools.partial(inner, steps, levels, width), grid=(step...  10 us
    pallas_call x1, Pallas kernels, run_outer(): pl.pallas_call(functools.partial(outer, steps, levels, width), grid=(step...  6.59 us
    ppermute x1, starting transfers between devices, shards(): right = lax.ppermute(first, 'lon', [(j, i) for i, j in up])  3.84 us
    unnamed x4, local copies, waits for them, and re-layouts  2.54 us
    another operation x1, other arithmetic, shards(): jnp.stack([p_speed, s_speed, density])  1.16 us
  transfers between devices with their start and end apart: 2, of which 0 were waited for; matrix products, arithmetic and copies ran while one was open for 0% of the time, Pallas kernels for 21%

profile of v4, /device:TPU:32, one launch (start us, length us, event | category | flops | bytes accessed | tf_op | source)
XLA Modules:
  0.0 47.8 jit_solution(5464259971055764003)
XLA Ops:
  0.0 1.2 %pad_maximum_fusion.material = f32[3,16,32,128]{3,2,1,0:T(8,128)S(1)} fusion(f32[1,16,32,128]{3,2,1,0:T(8,128)} %bitcast.7, f32[1,16,32,128]{3,2,1,0:T(8,128)} %bitcast.8, f32[1,16,32,128]{3,2,1,0:T(8,128)} %bitcast.9), kind=kLoop, calls=%fused_computation | loop fusion | flops 393216 | bytes 1572864 | tf_op jit(solution)/shard_map/stack | solution.py:360
  1.2 0.0 copy-start
  1.2 1.3 %copy-done = bf16[1,9,16,32,128]{4,3,2,1,0:T(8,128)(2,1)S(1)} copy-done((bf16[1,9,16,32,128]{4,3,2,1,0:T(8,128)(2,1)S(1)}, bf16[1,9,16,32,128]{4,3,2,1,0:T(8,128)(2,1)}, u32[]{:S(2)}) %copy-start) | copy-done | bytes 1179672
  2.4 0.2 shard_map.55
  2.7 0.1 collective-permute-start
  2.8 3.8 %collective-permute-start.1 = (bf16[12,16,8,128]{3,2,1,0:T(8,128)(2,1)S(1)}, bf16[12,16,8,128]{3,2,1,0:T(8,128)(2,1)S(1)}, u32[]{:S(2)}, u32[]{:S(2)}) collective-permute-start(bf16[12,16,8,128]{3,2,1,0:T(8,128)(2,1)S(1)} %get-tuple-element.13), channel_id=1, source_target_pairs={{1,0},{2,1},{3,2},{4,3},{5,4},{6,5},{7,6},{8,7},{9,8},{10,9},{11,1... | collective-permute-start | bytes 1179656 | tf_op jit(solution)/shard_map/ppermute | solution.py:364
  6.6 0.0 copy-start.1
  6.6 1.3 %copy-done.1 = bf16[1,9,16,32,128]{4,3,2,1,0:T(8,128)(2,1)S(1)} copy-done((bf16[1,9,16,32,128]{4,3,2,1,0:T(8,128)(2,1)S(1)}, bf16[1,9,16,32,128]{4,3,2,1,0:T(8,128)(2,1)}, u32[]{:S(2)}) %copy-start.1) | copy-done | bytes 1179672
  7.9 10.0 %shard_map.56 = (f32[3,16,32,128]{3,2,1,0:T(8,128)S(1)}, f32[2,9,16,16,128]{4,3,2,1,0:T(8,128)S(1)}, bf16[8,9,16,32,128]{4,3,2,1,0:T(8,128)(2,1)S(1)}) custom-call(bf16[9,16,32,128]{3,2,1,0:T(8,128)(2,1)S(1)} %bitcast.6, f32[3,16,32,128]{3,2,1,0:T(8,128)S(1)} %get-tuple-element.14.coef, bf16[1,8,9,16,32,128]{5,4,3,2,1,0:T(8,128)(2,1)} %forward_hbm.1), custom_call_target="tpu_custom_call" | custom-call | flops 60000000 | bytes 30000000 | tf_op jit(solution)/shard_map/pallas_call | solution.py:323
  17.9 0.0 collective-permute-done.left
  17.9 0.0 collective-permute-done.1.right
  17.9 6.6 %shard_map.57 = bf16[16,3,32,128]{3,2,1,0:T(8,128)(2,1)S(1)} custom-call(bf16[12,16,8,128]{3,2,1,0:T(8,128)(2,1)S(1)} %collective-permute-done.left, bf16[12,16,8,128]{3,2,1,0:T(8,128)(2,1)S(1)} %collective-permute-done.1.right, f32[3,16,32,128]{3,2,1,0:T(8,128)S(1)} %get-tuple-element.14.coef, bf16[8,9,16,32,128]{4,3,2,1,0:T(8,128)(2,1)S(1)} %get-tuple-element.15.forward, ...), custom_call_target="tpu_custom_call" | custom-call | flops 30000000 | bytes 20000000 | tf_op jit(solution)/shard_map/pallas_call | solution.py:340
  24.5 22.6 %all_to_all.5.parts = bf16[16,3,32,128]{3,2,1,0:T(8,128)(2,1)S(1)} all-to-all(bf16[16,3,32,128]{3,2,1,0:T(8,128)(2,1)S(1)} %shard_map.57), channel_id=1, replica_groups=mesh['event'=16,'lon'=16] {'event'}, dimensions={0} | all-to-all | bytes 786432 | tf_op jit(solution)/shard_map/all_to_all | solution.py:367
  47.1 0.7 %shard_map.58 = f32[3,1,32,128]{3,2,1,0:T(8,128)} custom-call(bf16[16,3,32,128]{3,2,1,0:T(8,128)(2,1)S(1)} %all_to_all.5.parts, f32[3,32,128]{2,1,0:T(8,128)S(1)} %get-tuple-element.18.own), custom_call_target="tpu_custom_call" | custom-call | tf_op jit(solution)/shard_map/pallas_call | solution.py:307
Async XLA Ops:
  1.2 1.3 %copy-start = (bf16[1,9,16,32,128]{4,3,2,1,0:T(8,128)(2,1)S(1)}, bf16[1,9,16,32,128]{4,3,2,1,0:T(8,128)(2,1)}, u32[]{:S(2)}) copy-start(bf16[1,9,16,32,128]{4,3,2,1,0:T(8,128)(2,1)} %param.5) | copy-start | bytes 3538948
  2.7 15.2 %collective-permute-start = (bf16[12,16,8,128]{3,2,1,0:T(8,128)(2,1)S(1)}, bf16[12,16,8,128]{3,2,1,0:T(8,128)(2,1)S(1)}, u32[]{:S(2)}, u32[]{:S(2)}) collective-permute-start(bf16[12,16,8,128]{3,2,1,0:T(8,128)(2,1)S(1)} %get-tuple-element.12), channel_id=1, source_target_pairs={{0,1},{1,2},{2,3},{3,4},{4,5},{5,6},{6,7},{7,8},{8,9},{9,10},{10,1... | collective-permute-start | bytes 1179656 | tf_op jit(solution)/shard_map/ppermute | solution.py:363
  2.8 15.2 %collective-permute-start.1 = (bf16[12,16,8,128]{3,2,1,0:T(8,128)(2,1)S(1)}, bf16[12,16,8,128]{3,2,1,0:T(8,128)(2,1)S(1)}, u32[]{:S(2)}, u32[]{:S(2)}) collective-permute-start(bf16[12,16,8,128]{3,2,1,0:T(8,128)(2,1)S(1)} %get-tuple-element.13), channel_id=1, source_target_pairs={{1,0},{2,1},{3,2},{4,3},{5,4},{6,5},{7,6},{8,7},{9,8},{10,9},{11,1... | collective-permute-start | bytes 1179656 | tf_op jit(solution)/shard_map/ppermute | solution.py:364
  6.6 1.3 %copy-start.1 = (bf16[1,9,16,32,128]{4,3,2,1,0:T(8,128)(2,1)S(1)}, bf16[1,9,16,32,128]{4,3,2,1,0:T(8,128)(2,1)}, u32[]{:S(2)}) copy-start(bf16[1,9,16,32,128]{4,3,2,1,0:T(8,128)(2,1)} %param.5) | copy-start | bytes 3538948

commit v5 on v4

--- a/solution.py
+++ b/solution.py
@@ -79,7 +79,7 @@
     )
 
 
-def inner(steps, levels, width, init, coef, forward_hbm, sums, stair, forward, state, arrived):
+def inner(steps, levels, width, half, init, coef, forward_hbm, sums, sent, kept, stair, forward, state, arrived):
     step = pl.program_id(0)
 
     def fetch(which):
@@ -151,6 +151,15 @@
         if level + 1 < levels:
             velocity(level + 1)
         stress(level)
+
+    @pl.when(step == steps - 1)
+    def _():
+        mine = pl.multiple_of(8 + 8 * half[0], 8)
+        other = pl.multiple_of(16 - 8 * half[0], 8)
+        for level in range(levels):
+            for which in range(3):
+                kept[which, level] = sums[which, level, pl.ds(mine, 8)]
+                sent[which, level] = sums[which, level, pl.ds(other, 8)].astype(BF16)
 
 
 def outer(steps, levels, width, left, right, coef, forward, first_sums, stair, out, state, mat, sums, wide_f):
@@ -239,39 +248,60 @@
 
     @pl.when(step == steps - 1)
     def _():
-        def store(level, carry):
-            for which, factor in enumerate((1.0, 2.0, 1.0)):
-                total = first_sums[which, level]
-                ends = [sums[side, which, level, pl.ds(8, 8)] for side in range(2)]
-                total = jnp.concatenate([total[:8] + ends[0], total[8:-8], total[-8:] + ends[1]])
-                out[level, which] = (factor * total).astype(BF16)
-            return carry
-
-        lax.fori_loop(0, levels, store, 0)
-
-
-def prepare(levels, width, row, init, material, first, last, coef, own):
-    def load(level, carry):
+        for level in range(levels):
+            for which in range(3):
+                for side, start in enumerate((0, width - 8)):
+                    out[side, which, level] = sums[side, which, level, pl.ds(8, 8)] + first_sums[which, level, pl.ds(start, 8)]
+
+
+def prepare(levels, width, row, init_hbm, material, first, last, init, coef, own, arrived):
+    copy = pltpu.make_async_copy(init_hbm, init, arrived.at[0])
+    copy.start()
+
+    def materials(level, carry):
         p, s, rho = [material[which, level] for which in range(3)]
         parts = (rho * (p * p - 2.0 * s * s), 2.0 * rho * s * s, 1.0 / rho)
         for which, part in enumerate(parts):
             coef[which, level] = part
             first[9 + which, level] = part[:HALO].astype(BF16)
             last[9 + which, level] = part[width - HALO :].astype(BF16)
+        return carry
+
+    lax.fori_loop(0, levels, materials, 0, unroll=4)
+    for which in range(3):
+        own[which] = material[which, row[0]]
+    copy.wait()
+
+    def edges(level, carry):
         for field in range(9):
             first[field, level] = init[field, level, pl.ds(0, 16)].astype(F32)[:HALO].astype(BF16)
             last[field, level] = init[field, level, pl.ds(width - 16, 16)].astype(F32)[16 - HALO :].astype(BF16)
         return carry
 
-    lax.fori_loop(0, levels, load, 0, unroll=4)
+    lax.fori_loop(0, levels, edges, 0, unroll=4)
+
+
+def join(levels, ends, kept, swapped, out):
+    for level in range(levels):
+        for which, factor in enumerate((1.0, 2.0, 1.0)):
+            quarter = kept[which, level] + swapped[which, level].astype(F32)
+            both = [ends[side, which, level] for side in range(2)]
+            out[level, which] = (factor * jnp.concatenate(both + [quarter])).astype(BF16)
+
+
+def finish(events, parts, own, out):
+    def summed(which, first, last):
+        total = parts[first, which].astype(F32)
+        for event in range(first + 1, last):
+            total = total + parts[event, which].astype(F32)
+        return total
+
+    half = events // 2
+    total = []
     for which in range(3):
-        own[which] = material[which, row[0]]
-
-
-def finish(events, parts, own, out):
-    total = [parts[0, which].astype(F32) for which in range(3)]
-    for event in range(1, events):
-        total = [so_far + parts[event, which].astype(F32) for which, so_far in enumerate(total)]
+        low, high = summed(which, 0, half), summed(which, half, events)
+        ends = low[:16] + high[:16]
+        total.append(jnp.concatenate([ends[:8], low[16:], high[16:], ends[8:]]))
     p_speed, s_speed, density = own[0], own[1], own[2]
     lame = density * (p_speed * p_speed - 2.0 * s_speed * s_speed)
     shear = density * s_speed * s_speed
@@ -290,20 +320,34 @@
     edge = jax.ShapeDtypeStruct((12, levels, HALO, lat), BF16)
     return pl.pallas_call(
         functools.partial(prepare, levels, width),
-        in_specs=[pl.BlockSpec(memory_space=pltpu.SMEM)] + [IN_VMEM] * 2,
-        out_specs=[IN_VMEM] * 4,
+        in_specs=[pl.BlockSpec(memory_space=pltpu.SMEM)] + [IN_HBM, IN_VMEM],
+        out_specs=[IN_VMEM] * 5,
         out_shape=[
             edge,
             edge,
+            jax.ShapeDtypeStruct(init.shape, BF16),
             jax.ShapeDtypeStruct((3, levels, width, lat), F32),
             jax.ShapeDtypeStruct((3, width, lat), F32),
         ],
-        compiler_params=pltpu.CompilerParams(vmem_limit_bytes=16 * MEBI),
+        scratch_shapes=[pltpu.SemaphoreType.DMA((1,))],
+        compiler_params=pltpu.CompilerParams(vmem_limit_bytes=50 * MEBI),
     )(row, init, material)
 
 
+def run_join(ends, kept, swapped):
+    _, levels, _, lat = kept.shape
+    return pl.pallas_call(
+        functools.partial(join, levels),
+        in_specs=[IN_VMEM] * 3,
+        out_specs=IN_VMEM,
+        out_shape=jax.ShapeDtypeStruct((levels, 3, 24, lat), BF16),
+        compiler_params=pltpu.CompilerParams(vmem_limit_bytes=8 * MEBI),
+    )(ends, kept, swapped)
+
+
 def run_finish(parts, own):
-    events, _, width, lat = parts.shape
+    events, _, _, lat = parts.shape
+    width = own.shape[1]
     return pl.pallas_call(
         functools.partial(finish, events),
         in_specs=[IN_VMEM] * 2,
@@ -313,18 +357,20 @@
     )(parts, own)
 
 
-def run_inner(init, coef, forward):
+def run_inner(half, init, coef, forward):
     _, steps, _, levels, width, lat = forward.shape
     outs = [
         jax.ShapeDtypeStruct((3, levels, width, lat), F32),
+        jax.ShapeDtypeStruct((3, levels, 8, lat), BF16),
+        jax.ShapeDtypeStruct((3, levels, 8, lat), F32),
         jax.ShapeDtypeStruct((2, 9, levels, 16, lat), F32),
         jax.ShapeDtypeStruct(forward.shape[1:], BF16),
     ]
     return pl.pallas_call(
         functools.partial(inner, steps, levels, width),
         grid=(steps,),
-        in_specs=[IN_VMEM, IN_VMEM, IN_HBM],
-        out_specs=[IN_VMEM] * 3,
+        in_specs=[pl.BlockSpec(memory_space=pltpu.SMEM), IN_VMEM, IN_VMEM, IN_HBM],
+        out_specs=[IN_VMEM] * 5,
         out_shape=outs,
         scratch_shapes=[
             pltpu.VMEM((9, levels + 2, width + 2 * PAD, lat), F32),
@@ -332,7 +378,7 @@
         ],
         compiler_params=pltpu.CompilerParams(vmem_limit_bytes=34 * MEBI),
         cost_estimate=pl.CostEstimate(flops=60_000_000, bytes_accessed=30_000_000, transcendentals=0),
-    )(init, coef, forward)
+    )(half, init, coef, forward)
 
 
 def run_outer(left, right, coef, forward, first_sums, stair):
@@ -342,7 +388,7 @@
         grid=(steps,),
         in_specs=[IN_VMEM] * 6,
         out_specs=IN_VMEM,
-        out_shape=jax.ShapeDtypeStruct((levels, 3, width, lat), BF16),
+        out_shape=jax.ShapeDtypeStruct((2, 3, levels, 8, lat), F32),
         scratch_shapes=[
             pltpu.VMEM((2, 9, levels + 2, 24, lat), F32),
             pltpu.VMEM((2, 3, levels, 24, lat), F32),
@@ -357,13 +403,17 @@
 def shards(adjoint_init, forward_state, p_speed, s_speed, density):
     init = adjoint_init[0]
     row = lax.axis_index("event").reshape(1)
-    first, last, coef, own = run_prepare(row, init, jnp.stack([p_speed, s_speed, density]))
+    first, last, init, coef, own = run_prepare(row, init, jnp.stack([p_speed, s_speed, density]))
     count = lax.axis_size("lon")
     up = [(i, (i + 1) % count) for i in range(count)]
     left = lax.ppermute(last, "lon", up)
     right = lax.ppermute(first, "lon", [(j, i) for i, j in up])
-    first_sums, stair, forward = run_inner(init, coef, forward_state)
-    partial = run_outer(left, right, coef, forward, first_sums, stair)
+    pairs = lax.axis_size("event") // 2
+    first_sums, sent, kept, stair, forward = run_inner(row // pairs, init, coef, forward_state)
+    swap = [(i, (i + pairs) % (2 * pairs)) for i in range(2 * pairs)]
+    swapped = lax.ppermute(sent, "event", swap)
+    ends = run_outer(left, right, coef, forward, first_sums, stair)
+    partial = run_join(ends, kept, swapped)
     parts = lax.all_to_all(partial, "event", 0, 0, tiled=True)
     return run_finish(parts, own)
 

time: 48.1 us -> 46.7 us (0.971)
  blocking collectives: 22.6 us -> 19.2 us
  starting transfers between devices: 3.93 us -> 7.04 us
  local copies, waits for them, and re-layouts: 2.54 us -> 0 us
  Pallas kernels: 17.5 us -> 19.2 us
    all_to_all x1, blocking collectives: 22.6 us -> 19.2 us  [shards(): parts = lax.all_to_all(partial, 'event', 0, 0, tiled=True)]
    ppermute x0 -> x1, starting transfers between devices: none -> 3.11 us  [shards(): swapped = lax.ppermute(sent, 'event', swap)]
    unnamed x4 -> x0, local copies, waits for them, and re-layouts: 2.54 us -> none
    pallas_call x1, Pallas kernels: 0.24 us -> 1.44 us  [run_prepare(): pl.pallas_call(functools.partial(prepare, levels, width), in_specs=[pl.Bl...]
  transfers between devices with their start and end apart: 2 -> 3, of which waited for: 0 -> 0; matrix products, arithmetic and copies ran while one was open for 0% -> 0% of each run, Pallas kernels for 21% -> 36%
where the time goes in v5:
time: 46.7 us; the launch traced here: 46.6 us
  Pallas kernels  19.2 us (41%)
  blocking collectives  19.2 us (41%)
  starting transfers between devices  7.04 us (15%)
  other arithmetic  1.16 us (2%)
    all_to_all x1, blocking collectives, shards(): parts = lax.all_to_all(partial, 'event', 0, 0, tiled=True)  19.2 us
    pallas_call x1, Pallas kernels, run_inner(): pl.pallas_call(functools.partial(inner, steps, levels, width), grid=(step...  10.3 us
    pallas_call x1, Pallas kernels, run_outer(): pl.pallas_call(functools.partial(outer, steps, levels, width), grid=(step...  6.67 us
    ppermute x1, starting transfers between devices, shards(): right = lax.ppermute(first, 'lon', [(j, i) for i, j in up])  3.84 us
    ppermute x1, starting transfers between devices, shards(): swapped = lax.ppermute(sent, 'event', swap)  3.11 us
    pallas_call x1, Pallas kernels, run_prepare(): pl.pallas_call(functools.partial(prepare, levels, width), in_specs=[pl.Bl...  1.44 us
    another operation x1, other arithmetic, shards(): jnp.stack([p_speed, s_speed, density])  1.16 us
  transfers between devices with their start and end apart: 3, of which 0 were waited for; matrix products, arithmetic and copies ran while one was open for 0% of the time, Pallas kernels for 36%

profile of v5, /device:TPU:32, one launch (start us, length us, event | category | flops | bytes accessed | tf_op | source)
XLA Modules:
  0.0 46.6 jit_solution(11052488350402504108)
XLA Ops:
  0.0 1.2 %pad_maximum_fusion.material = f32[3,16,32,128]{3,2,1,0:T(8,128)S(1)} fusion(f32[1,16,32,128]{3,2,1,0:T(8,128)} %bitcast.6, f32[1,16,32,128]{3,2,1,0:T(8,128)} %bitcast.7, f32[1,16,32,128]{3,2,1,0:T(8,128)} %bitcast.8), kind=kLoop, calls=%fused_computation | loop fusion | flops 393216 | bytes 1572864 | tf_op jit(solution)/shard_map/stack | solution.py:406
  1.2 1.4 %shard_map.55 = (bf16[12,16,8,128]{3,2,1,0:T(8,128)(2,1)S(1)}, bf16[12,16,8,128]{3,2,1,0:T(8,128)(2,1)S(1)}, bf16[9,16,32,128]{3,2,1,0:T(8,128)(2,1)S(1)}, f32[3...) custom-call(s32[1]{0:T(128)} %bitcast.row, bf16[9,16,32,128]{3,2,1,0:T(8,128)(2,1)} %bitcast.5, ...), custom_call_target="tpu_custom_call" | custom-call | tf_op jit(solution)/shard_map/pallas_call | solution.py:321
  2.6 0.1 collective-permute-start
  2.7 3.8 %collective-permute-start.1 = (bf16[12,16,8,128]{3,2,1,0:T(8,128)(2,1)S(1)}, bf16[12,16,8,128]{3,2,1,0:T(8,128)(2,1)S(1)}, u32[]{:S(2)}, u32[]{:S(2)}) collective-permute-start(bf16[12,16,8,128]{3,2,1,0:T(8,128)(2,1)S(1)} %get-tuple-element.16), channel_id=1, source_target_pairs={{1,0},{2,1},{3,2},{4,3},{5,4},{6,5},{7,6},{8,7},{9,8},{10,9},{11,1... | collective-permute-start | bytes 1179656 | tf_op jit(solution)/shard_map/ppermute | solution.py:410
  6.5 10.3 %shard_map.56 = (f32[3,16,32,128]{3,2,1,0:T(8,128)S(1)}, bf16[3,16,8,128]{3,2,1,0:T(8,128)(2,1)S(1)}, f32[3,16,8,128]{3,2,1,0:T(8,128)S(1)}, f32[2,9,16,16,128]{...) custom-call(s32[1]{0:T(128)S(6)} %select_n.5.half, bf16[9,16,32,128]{3,2,1,0:T(8,128)(2,1)S(1)} %get-tuple-element.18.init, ...), custom_call_target="tpu_custom_call" | custom-call | flops 60000000 | bytes 30000000 | tf_op jit(solution)/shard_map/pallas_call | solution.py:369
  16.9 3.1 %collective-permute-start.2 = (bf16[3,16,8,128]{3,2,1,0:T(8,128)(2,1)S(1)}, bf16[3,16,8,128]{3,2,1,0:T(8,128)(2,1)S(1)}, u32[]{:S(2)}, u32[]{:S(2)}) collective-permute-start(bf16[3,16,8,128]{3,2,1,0:T(8,128)(2,1)S(1)} %get-tuple-element.23), channel_id=1, source_target_pairs={{0,128},{16,144},{32,160},{48,176},{64,192},{80,208},{96,224},{112... | collective-permute-start | bytes 294920 | tf_op jit(solution)/shard_map/ppermute | solution.py:414
  20.0 0.0 collective-permute-done.left
  20.0 0.0 collective-permute-done.1.right
  20.0 6.7 %shard_map.57.ends = f32[2,3,16,8,128]{4,3,2,1,0:T(8,128)S(1)} custom-call(bf16[12,16,8,128]{3,2,1,0:T(8,128)(2,1)S(1)} %collective-permute-done.left, bf16[12,16,8,128]{3,2,1,0:T(8,128)(2,1)S(1)} %collective-permute-done.1.right, f32[3,16,32,128]{3,2,1,0:T(8,128)S(1)} %get-tuple-element.17.coef, bf16[8,9,16,32,128]{4,3,2,1,0:T(8,128)(2,1)S(1)} %get-tuple-element.19.forward, ...), custom_call_target="tpu_custom_call" | custom-call | flops 30000000 | bytes 20000000 | tf_op jit(solution)/shard_map/pallas_call | solution.py:386
  26.7 0.0 collective-permute-done.2.swapped
  26.7 0.1 shard_map.58
  26.7 19.2 %all_to_all.5.parts = bf16[16,3,24,128]{3,2,1,0:T(8,128)(2,1)S(1)} all-to-all(bf16[16,3,24,128]{3,2,1,0:T(8,128)(2,1)S(1)} %shard_map.58), channel_id=1, replica_groups=mesh['event'=16,'lon'=16] {'event'}, dimensions={0} | all-to-all | bytes 589824 | tf_op jit(solution)/shard_map/all_to_all | solution.py:417
  45.9 0.7 %shard_map.59 = f32[3,1,32,128]{3,2,1,0:T(8,128)} custom-call(bf16[16,3,24,128]{3,2,1,0:T(8,128)(2,1)S(1)} %all_to_all.5.parts, f32[3,32,128]{2,1,0:T(8,128)S(1)} %get-tuple-element.24.own), custom_call_target="tpu_custom_call" | custom-call | tf_op jit(solution)/shard_map/pallas_call | solution.py:351
Async XLA Ops:
  2.6 17.4 %collective-permute-start = (bf16[12,16,8,128]{3,2,1,0:T(8,128)(2,1)S(1)}, bf16[12,16,8,128]{3,2,1,0:T(8,128)(2,1)S(1)}, u32[]{:S(2)}, u32[]{:S(2)}) collective-permute-start(bf16[12,16,8,128]{3,2,1,0:T(8,128)(2,1)S(1)} %get-tuple-element.15), channel_id=1, source_target_pairs={{0,1},{1,2},{2,3},{3,4},{4,5},{5,6},{6,7},{7,8},{8,9},{9,10},{10,1... | collective-permute-start | bytes 1179656 | tf_op jit(solution)/shard_map/ppermute | solution.py:409
  2.7 17.3 %collective-permute-start.1 = (bf16[12,16,8,128]{3,2,1,0:T(8,128)(2,1)S(1)}, bf16[12,16,8,128]{3,2,1,0:T(8,128)(2,1)S(1)}, u32[]{:S(2)}, u32[]{:S(2)}) collective-permute-start(bf16[12,16,8,128]{3,2,1,0:T(8,128)(2,1)S(1)} %get-tuple-element.16), channel_id=1, source_target_pairs={{1,0},{2,1},{3,2},{4,3},{5,4},{6,5},{7,6},{8,7},{9,8},{10,9},{11,1... | collective-permute-start | bytes 1179656 | tf_op jit(solution)/shard_map/ppermute | solution.py:410
  16.9 9.8 %collective-permute-start.2 = (bf16[3,16,8,128]{3,2,1,0:T(8,128)(2,1)S(1)}, bf16[3,16,8,128]{3,2,1,0:T(8,128)(2,1)S(1)}, u32[]{:S(2)}, u32[]{:S(2)}) collective-permute-start(bf16[3,16,8,128]{3,2,1,0:T(8,128)(2,1)S(1)} %get-tuple-element.23), channel_id=1, source_target_pairs={{0,128},{16,144},{32,160},{48,176},{64,192},{80,208},{96,224},{112... | collective-permute-start | bytes 294920 | tf_op jit(solution)/shard_map/ppermute | solution.py:414

commit v6 on v5

--- a/solution.py
+++ b/solution.py
@@ -82,16 +82,20 @@
 def inner(steps, levels, width, half, init, coef, forward_hbm, sums, sent, kept, stair, forward, state, arrived):
     step = pl.program_id(0)
 
-    def fetch(which):
-        return pltpu.make_async_copy(forward_hbm.at[0, which], forward.at[which], arrived.at[which])
+    starts = (0, 2)
+
+    def fetch(group):
+        begin = starts[group]
+        part = pl.ds(begin, (starts + (steps,))[group + 1] - begin)
+        return pltpu.make_async_copy(forward_hbm.at[0, part], forward.at[part], arrived.at[group])
 
     def keep(level, side, field, row, value):
         stair[side, field, level, pl.ds(row, 1)] = value
 
     @pl.when(step == 0)
     def _():
-        for which in range(steps):
-            fetch(which).start()
+        for group in range(len(starts)):
+            fetch(group).start()
         empty = jnp.zeros((9, 1, width + 2 * PAD, 128), F32)
         state[:, pl.ds(0, 1)] = empty
         state[:, pl.ds(levels + 1, 1)] = empty
@@ -137,15 +141,20 @@
             mine = pl.ds(start, 16)
             parts = strain(*view(level, start, 16), coef[LAME, level, mine], coef[SHEAR2, level, mine])
             f = [forward[step, field, level, mine].astype(F32) for field in range(9)]
-            column = start + lax.broadcasted_iota(jnp.int32, (16, 128), 0)
-            right = (column > step) & (column < width - 1 - step)
+            column = lax.broadcasted_iota(jnp.int32, (8, 128), 0)
             for which, term in enumerate(terms(*parts, f)):
-                sums[which, level, mine] += jnp.where(right, term, 0.0)
+                if start == 0:
+                    term = jnp.concatenate([jnp.where(column > step, term[:8], 0.0), term[8:]])
+                elif start == width - 16:
+                    term = jnp.concatenate([term[:8], jnp.where(column < 7 - step, term[8:], 0.0)])
+                sums[which, level, mine] += term
         for field in range(3, 9):
             keep(level, 0, field, step + 1, state[field, level + 1, pl.ds(PAD + step + 1, 1)])
             keep(level, 1, field, 14 - step, state[field, level + 1, pl.ds(PAD + 30 - step, 1)])
 
-    fetch(step).wait()
+    for group, begin in enumerate(starts):
+        pl.when(step == begin)(fetch(group).wait)
+
     velocity(0)
     for level in range(levels):
         if level + 1 < levels:
@@ -374,7 +383,7 @@
         out_shape=outs,
         scratch_shapes=[
             pltpu.VMEM((9, levels + 2, width + 2 * PAD, lat), F32),
-            pltpu.SemaphoreType.DMA((steps,)),
+            pltpu.SemaphoreType.DMA((2,)),
         ],
         compiler_params=pltpu.CompilerParams(vmem_limit_bytes=34 * MEBI),
         cost_estimate=pl.CostEstimate(flops=60_000_000, bytes_accessed=30_000_000, transcendentals=0),

time: 46.7 us -> 47 us (level)
  transfers between devices with their start and end apart: 3 -> 3, of which waited for: 0 -> 0; matrix products, arithmetic and copies ran while one was open for 0% -> 0% of each run, Pallas kernels for 36% -> 37%
where the time goes in v6:
time: 47 us; the launch traced here: 46.8 us
  Pallas kernels  19.4 us (41%)
  blocking collectives  19.2 us (41%)
  starting transfers between devices  7.04 us (15%)
  other arithmetic  1.16 us (2%)
    all_to_all x1, blocking collectives, shards(): parts = lax.all_to_all(partial, 'event', 0, 0, tiled=True)  19.2 us
    pallas_call x1, Pallas kernels, run_inner(): pl.pallas_call(functools.partial(inner, steps, levels, width), grid=(step...  10.6 us
    pallas_call x1, Pallas kernels, run_outer(): pl.pallas_call(functools.partial(outer, steps, levels, width), grid=(step...  6.67 us
    ppermute x1, starting transfers between devices, shards(): right = lax.ppermute(first, 'lon', [(j, i) for i, j in up])  3.84 us
    ppermute x1, starting transfers between devices, shards(): swapped = lax.ppermute(sent, 'event', swap)  3.11 us
    pallas_call x1, Pallas kernels, run_prepare(): pl.pallas_call(functools.partial(prepare, levels, width), in_specs=[pl.Bl...  1.44 us
    another operation x1, other arithmetic, shards(): jnp.stack([p_speed, s_speed, density])  1.16 us
  transfers between devices with their start and end apart: 3, of which 0 were waited for; matrix products, arithmetic and copies ran while one was open for 0% of the time, Pallas kernels for 37%

profile of v6, /device:TPU:32, one launch (start us, length us, event | category | flops | bytes accessed | tf_op | source)
XLA Modules:
  0.0 46.8 jit_solution(11679209097499922396)
XLA Ops:
  0.0 1.2 %pad_maximum_fusion.material = f32[3,16,32,128]{3,2,1,0:T(8,128)S(1)} fusion(f32[1,16,32,128]{3,2,1,0:T(8,128)} %bitcast.6, f32[1,16,32,128]{3,2,1,0:T(8,128)} %bitcast.7, f32[1,16,32,128]{3,2,1,0:T(8,128)} %bitcast.8), kind=kLoop, calls=%fused_computation | loop fusion | flops 393216 | bytes 1572864 | tf_op jit(solution)/shard_map/stack | solution.py:415
  1.2 1.4 %shard_map.55 = (bf16[12,16,8,128]{3,2,1,0:T(8,128)(2,1)S(1)}, bf16[12,16,8,128]{3,2,1,0:T(8,128)(2,1)S(1)}, bf16[9,16,32,128]{3,2,1,0:T(8,128)(2,1)S(1)}, f32[3...) custom-call(s32[1]{0:T(128)} %bitcast.row, bf16[9,16,32,128]{3,2,1,0:T(8,128)(2,1)} %bitcast.5, ...), custom_call_target="tpu_custom_call" | custom-call | tf_op jit(solution)/shard_map/pallas_call | solution.py:330
  2.6 0.1 collective-permute-start
  2.7 3.8 %collective-permute-start.1 = (bf16[12,16,8,128]{3,2,1,0:T(8,128)(2,1)S(1)}, bf16[12,16,8,128]{3,2,1,0:T(8,128)(2,1)S(1)}, u32[]{:S(2)}, u32[]{:S(2)}) collective-permute-start(bf16[12,16,8,128]{3,2,1,0:T(8,128)(2,1)S(1)} %get-tuple-element.16), channel_id=1, source_target_pairs={{1,0},{2,1},{3,2},{4,3},{5,4},{6,5},{7,6},{8,7},{9,8},{10,9},{11,1... | collective-permute-start | bytes 1179656 | tf_op jit(solution)/shard_map/ppermute | solution.py:419
  6.5 10.6 %shard_map.56 = (f32[3,16,32,128]{3,2,1,0:T(8,128)S(1)}, bf16[3,16,8,128]{3,2,1,0:T(8,128)(2,1)S(1)}, f32[3,16,8,128]{3,2,1,0:T(8,128)S(1)}, f32[2,9,16,16,128]{...) custom-call(s32[1]{0:T(128)S(6)} %select_n.5.half, bf16[9,16,32,128]{3,2,1,0:T(8,128)(2,1)S(1)} %get-tuple-element.18.init, ...), custom_call_target="tpu_custom_call" | custom-call | flops 60000000 | bytes 30000000 | tf_op jit(solution)/shard_map/pallas_call | solution.py:378
  17.1 3.1 %collective-permute-start.2 = (bf16[3,16,8,128]{3,2,1,0:T(8,128)(2,1)S(1)}, bf16[3,16,8,128]{3,2,1,0:T(8,128)(2,1)S(1)}, u32[]{:S(2)}, u32[]{:S(2)}) collective-permute-start(bf16[3,16,8,128]{3,2,1,0:T(8,128)(2,1)S(1)} %get-tuple-element.23), channel_id=1, source_target_pairs={{0,128},{16,144},{32,160},{48,176},{64,192},{80,208},{96,224},{112... | collective-permute-start | bytes 294920 | tf_op jit(solution)/shard_map/ppermute | solution.py:423
  20.2 0.0 collective-permute-done.left
  20.2 0.0 collective-permute-done.1.right
  20.2 6.7 %shard_map.57.ends = f32[2,3,16,8,128]{4,3,2,1,0:T(8,128)S(1)} custom-call(bf16[12,16,8,128]{3,2,1,0:T(8,128)(2,1)S(1)} %collective-permute-done.left, bf16[12,16,8,128]{3,2,1,0:T(8,128)(2,1)S(1)} %collective-permute-done.1.right, f32[3,16,32,128]{3,2,1,0:T(8,128)S(1)} %get-tuple-element.17.coef, bf16[8,9,16,32,128]{4,3,2,1,0:T(8,128)(2,1)S(1)} %get-tuple-element.19.forward, ...), custom_call_target="tpu_custom_call" | custom-call | flops 30000000 | bytes 20000000 | tf_op jit(solution)/shard_map/pallas_call | solution.py:395
  26.9 0.0 collective-permute-done.2.swapped
  26.9 0.1 shard_map.58
  27.0 19.2 %all_to_all.5.parts = bf16[16,3,24,128]{3,2,1,0:T(8,128)(2,1)S(1)} all-to-all(bf16[16,3,24,128]{3,2,1,0:T(8,128)(2,1)S(1)} %shard_map.58), channel_id=1, replica_groups=mesh['event'=16,'lon'=16] {'event'}, dimensions={0} | all-to-all | bytes 589824 | tf_op jit(solution)/shard_map/all_to_all | solution.py:426
  46.1 0.7 %shard_map.59 = f32[3,1,32,128]{3,2,1,0:T(8,128)} custom-call(bf16[16,3,24,128]{3,2,1,0:T(8,128)(2,1)S(1)} %all_to_all.5.parts, f32[3,32,128]{2,1,0:T(8,128)S(1)} %get-tuple-element.24.own), custom_call_target="tpu_custom_call" | custom-call | tf_op jit(solution)/shard_map/pallas_call | solution.py:360
Async XLA Ops:
  2.6 17.6 %collective-permute-start = (bf16[12,16,8,128]{3,2,1,0:T(8,128)(2,1)S(1)}, bf16[12,16,8,128]{3,2,1,0:T(8,128)(2,1)S(1)}, u32[]{:S(2)}, u32[]{:S(2)}) collective-permute-start(bf16[12,16,8,128]{3,2,1,0:T(8,128)(2,1)S(1)} %get-tuple-element.15), channel_id=1, source_target_pairs={{0,1},{1,2},{2,3},{3,4},{4,5},{5,6},{6,7},{7,8},{8,9},{9,10},{10,1... | collective-permute-start | bytes 1179656 | tf_op jit(solution)/shard_map/ppermute | solution.py:418
  2.7 17.5 %collective-permute-start.1 = (bf16[12,16,8,128]{3,2,1,0:T(8,128)(2,1)S(1)}, bf16[12,16,8,128]{3,2,1,0:T(8,128)(2,1)S(1)}, u32[]{:S(2)}, u32[]{:S(2)}) collective-permute-start(bf16[12,16,8,128]{3,2,1,0:T(8,128)(2,1)S(1)} %get-tuple-element.16), channel_id=1, source_target_pairs={{1,0},{2,1},{3,2},{4,3},{5,4},{6,5},{7,6},{8,7},{9,8},{10,9},{11,1... | collective-permute-start | bytes 1179656 | tf_op jit(solution)/shard_map/ppermute | solution.py:419
  17.1 9.8 %collective-permute-start.2 = (bf16[3,16,8,128]{3,2,1,0:T(8,128)(2,1)S(1)}, bf16[3,16,8,128]{3,2,1,0:T(8,128)(2,1)S(1)}, u32[]{:S(2)}, u32[]{:S(2)}) collective-permute-start(bf16[3,16,8,128]{3,2,1,0:T(8,128)(2,1)S(1)} %get-tuple-element.23), channel_id=1, source_target_pairs={{0,128},{16,144},{32,160},{48,176},{64,192},{80,208},{96,224},{112... | collective-permute-start | bytes 294920 | tf_op jit(solution)/shard_map/ppermute | solution.py:423

commit v7 on v6

--- a/solution.py
+++ b/solution.py
@@ -82,7 +82,7 @@
 def inner(steps, levels, width, half, init, coef, forward_hbm, sums, sent, kept, stair, forward, state, arrived):
     step = pl.program_id(0)
 
-    starts = (0, 2)
+    starts = (0, 1, 3)
 
     def fetch(group):
         begin = starts[group]
@@ -94,8 +94,7 @@
 
     @pl.when(step == 0)
     def _():
-        for group in range(len(starts)):
-            fetch(group).start()
+        fetch(0).start()
         empty = jnp.zeros((9, 1, width + 2 * PAD, 128), F32)
         state[:, pl.ds(0, 1)] = empty
         state[:, pl.ds(levels + 1, 1)] = empty
@@ -116,6 +115,8 @@
             return carry
 
         lax.fori_loop(0, levels, load, 0)
+        for group in range(1, len(starts)):
+            fetch(group).start()
 
     def view(level, start, rows):
         def at(field, lev, lon):
@@ -383,7 +384,7 @@
         out_shape=outs,
         scratch_shapes=[
             pltpu.VMEM((9, levels + 2, width + 2 * PAD, lat), F32),
-            pltpu.SemaphoreType.DMA((2,)),
+            pltpu.SemaphoreType.DMA((3,)),
         ],
         compiler_params=pltpu.CompilerParams(vmem_limit_bytes=34 * MEBI),
         cost_estimate=pl.CostEstimate(flops=60_000_000, bytes_accessed=30_000_000, transcendentals=0),

time: 47 us -> 46.6 us (level)
  transfers between devices with their start and end apart: 3 -> 3, of which waited for: 0 -> 0; matrix products, arithmetic and copies ran while one was open for 0% -> 0% of each run, Pallas kernels for 37% -> 36%
where the time goes in v7:
time: 46.6 us; the launch traced here: 46.4 us
  blocking collectives  19.2 us (41%)
  Pallas kernels  19 us (41%)
  starting transfers between devices  7.04 us (15%)
  other arithmetic  1.16 us (2%)
    all_to_all x1, blocking collectives, shards(): parts = lax.all_to_all(partial, 'event', 0, 0, tiled=True)  19.2 us
    pallas_call x1, Pallas kernels, run_inner(): pl.pallas_call(functools.partial(inner, steps, levels, width), grid=(step...  10.2 us
    pallas_call x1, Pallas kernels, run_outer(): pl.pallas_call(functools.partial(outer, steps, levels, width), grid=(step...  6.67 us
    ppermute x1, starting transfers between devices, shards(): right = lax.ppermute(first, 'lon', [(j, i) for i, j in up])  3.84 us
    ppermute x1, starting transfers between devices, shards(): swapped = lax.ppermute(sent, 'event', swap)  3.11 us
    pallas_call x1, Pallas kernels, run_prepare(): pl.pallas_call(functools.partial(prepare, levels, width), in_specs=[pl.Bl...  1.44 us
    another operation x1, other arithmetic, shards(): jnp.stack([p_speed, s_speed, density])  1.16 us
  transfers between devices with their start and end apart: 3, of which 0 were waited for; matrix products, arithmetic and copies ran while one was open for 0% of the time, Pallas kernels for 36%

profile of v7, /device:TPU:32, one launch (start us, length us, event | category | flops | bytes accessed | tf_op | source)
XLA Modules:
  0.0 46.4 jit_solution(11140776568059632030)
XLA Ops:
  0.0 1.2 %pad_maximum_fusion.material = f32[3,16,32,128]{3,2,1,0:T(8,128)S(1)} fusion(f32[1,16,32,128]{3,2,1,0:T(8,128)} %bitcast.6, f32[1,16,32,128]{3,2,1,0:T(8,128)} %bitcast.7, f32[1,16,32,128]{3,2,1,0:T(8,128)} %bitcast.8), kind=kLoop, calls=%fused_computation | loop fusion | flops 393216 | bytes 1572864 | tf_op jit(solution)/shard_map/stack | solution.py:416
  1.2 1.4 %shard_map.55 = (bf16[12,16,8,128]{3,2,1,0:T(8,128)(2,1)S(1)}, bf16[12,16,8,128]{3,2,1,0:T(8,128)(2,1)S(1)}, bf16[9,16,32,128]{3,2,1,0:T(8,128)(2,1)S(1)}, f32[3...) custom-call(s32[1]{0:T(128)} %bitcast.row, bf16[9,16,32,128]{3,2,1,0:T(8,128)(2,1)} %bitcast.5, ...), custom_call_target="tpu_custom_call" | custom-call | tf_op jit(solution)/shard_map/pallas_call | solution.py:331
  2.6 0.1 collective-permute-start
  2.7 3.8 %collective-permute-start.1 = (bf16[12,16,8,128]{3,2,1,0:T(8,128)(2,1)S(1)}, bf16[12,16,8,128]{3,2,1,0:T(8,128)(2,1)S(1)}, u32[]{:S(2)}, u32[]{:S(2)}) collective-permute-start(bf16[12,16,8,128]{3,2,1,0:T(8,128)(2,1)S(1)} %get-tuple-element.16), channel_id=1, source_target_pairs={{1,0},{2,1},{3,2},{4,3},{5,4},{6,5},{7,6},{8,7},{9,8},{10,9},{11,1... | collective-permute-start | bytes 1179656 | tf_op jit(solution)/shard_map/ppermute | solution.py:420
  6.5 10.2 %shard_map.56 = (f32[3,16,32,128]{3,2,1,0:T(8,128)S(1)}, bf16[3,16,8,128]{3,2,1,0:T(8,128)(2,1)S(1)}, f32[3,16,8,128]{3,2,1,0:T(8,128)S(1)}, f32[2,9,16,16,128]{...) custom-call(s32[1]{0:T(128)S(6)} %select_n.5.half, bf16[9,16,32,128]{3,2,1,0:T(8,128)(2,1)S(1)} %get-tuple-element.18.init, ...), custom_call_target="tpu_custom_call" | custom-call | flops 60000000 | bytes 30000000 | tf_op jit(solution)/shard_map/pallas_call | solution.py:379
  16.7 3.1 %collective-permute-start.2 = (bf16[3,16,8,128]{3,2,1,0:T(8,128)(2,1)S(1)}, bf16[3,16,8,128]{3,2,1,0:T(8,128)(2,1)S(1)}, u32[]{:S(2)}, u32[]{:S(2)}) collective-permute-start(bf16[3,16,8,128]{3,2,1,0:T(8,128)(2,1)S(1)} %get-tuple-element.23), channel_id=1, source_target_pairs={{0,128},{16,144},{32,160},{48,176},{64,192},{80,208},{96,224},{112... | collective-permute-start | bytes 294920 | tf_op jit(solution)/shard_map/ppermute | solution.py:424
  19.8 0.0 collective-permute-done.left
  19.8 0.0 collective-permute-done.1.right
  19.8 6.7 %shard_map.57.ends = f32[2,3,16,8,128]{4,3,2,1,0:T(8,128)S(1)} custom-call(bf16[12,16,8,128]{3,2,1,0:T(8,128)(2,1)S(1)} %collective-permute-done.left, bf16[12,16,8,128]{3,2,1,0:T(8,128)(2,1)S(1)} %collective-permute-done.1.right, f32[3,16,32,128]{3,2,1,0:T(8,128)S(1)} %get-tuple-element.17.coef, bf16[8,9,16,32,128]{4,3,2,1,0:T(8,128)(2,1)S(1)} %get-tuple-element.19.forward, ...), custom_call_target="tpu_custom_call" | custom-call | flops 30000000 | bytes 20000000 | tf_op jit(solution)/shard_map/pallas_call | solution.py:396
  26.5 0.0 collective-permute-done.2.swapped
  26.5 0.1 shard_map.58
  26.6 19.2 %all_to_all.5.parts = bf16[16,3,24,128]{3,2,1,0:T(8,128)(2,1)S(1)} all-to-all(bf16[16,3,24,128]{3,2,1,0:T(8,128)(2,1)S(1)} %shard_map.58), channel_id=1, replica_groups=mesh['event'=16,'lon'=16] {'event'}, dimensions={0} | all-to-all | bytes 589824 | tf_op jit(solution)/shard_map/all_to_all | solution.py:427
  45.8 0.7 %shard_map.59 = f32[3,1,32,128]{3,2,1,0:T(8,128)} custom-call(bf16[16,3,24,128]{3,2,1,0:T(8,128)(2,1)S(1)} %all_to_all.5.parts, f32[3,32,128]{2,1,0:T(8,128)S(1)} %get-tuple-element.24.own), custom_call_target="tpu_custom_call" | custom-call | tf_op jit(solution)/shard_map/pallas_call | solution.py:361
Async XLA Ops:
  2.6 17.2 %collective-permute-start = (bf16[12,16,8,128]{3,2,1,0:T(8,128)(2,1)S(1)}, bf16[12,16,8,128]{3,2,1,0:T(8,128)(2,1)S(1)}, u32[]{:S(2)}, u32[]{:S(2)}) collective-permute-start(bf16[12,16,8,128]{3,2,1,0:T(8,128)(2,1)S(1)} %get-tuple-element.15), channel_id=1, source_target_pairs={{0,1},{1,2},{2,3},{3,4},{4,5},{5,6},{6,7},{7,8},{8,9},{9,10},{10,1... | collective-permute-start | bytes 1179656 | tf_op jit(solution)/shard_map/ppermute | solution.py:419
  2.7 17.1 %collective-permute-start.1 = (bf16[12,16,8,128]{3,2,1,0:T(8,128)(2,1)S(1)}, bf16[12,16,8,128]{3,2,1,0:T(8,128)(2,1)S(1)}, u32[]{:S(2)}, u32[]{:S(2)}) collective-permute-start(bf16[12,16,8,128]{3,2,1,0:T(8,128)(2,1)S(1)} %get-tuple-element.16), channel_id=1, source_target_pairs={{1,0},{2,1},{3,2},{4,3},{5,4},{6,5},{7,6},{8,7},{9,8},{10,9},{11,1... | collective-permute-start | bytes 1179656 | tf_op jit(solution)/shard_map/ppermute | solution.py:420
  16.7 9.8 %collective-permute-start.2 = (bf16[3,16,8,128]{3,2,1,0:T(8,128)(2,1)S(1)}, bf16[3,16,8,128]{3,2,1,0:T(8,128)(2,1)S(1)}, u32[]{:S(2)}, u32[]{:S(2)}) collective-permute-start(bf16[3,16,8,128]{3,2,1,0:T(8,128)(2,1)S(1)} %get-tuple-element.23), channel_id=1, source_target_pairs={{0,128},{16,144},{32,160},{48,176},{64,192},{80,208},{96,224},{112... | collective-permute-start | bytes 294920 | tf_op jit(solution)/shard_map/ppermute | solution.py:424

commit v8 on v7

--- a/solution.py
+++ b/solution.py
@@ -104,8 +104,6 @@
                 state[field, level + 1, pl.ds(0, PAD)] = jnp.zeros((PAD, 128), F32)
                 state[field, level + 1, pl.ds(PAD + width, PAD)] = jnp.zeros((PAD, 128), F32)
                 state[field, level + 1, pl.ds(PAD, width)] = init[field, level].astype(F32)
-                stair[0, field, level] = jnp.zeros((16, 128), F32)
-                stair[1, field, level] = jnp.zeros((16, 128), F32)
                 if field != VX:
                     stair[0, field, level, pl.ds(0, 1)] = state[field, level + 1, pl.ds(PAD, 1)]
                 if field not in (VY, VZ):

time: 46.6 us -> 46.6 us (level)
  no operation moved by 1% of the time
where the time goes in v8:
time: 46.6 us; the launch traced here: 46.4 us
  blocking collectives  19.2 us (41%)
  Pallas kernels  19 us (41%)
  starting transfers between devices  7.04 us (15%)
  other arithmetic  1.16 us (2%)
    all_to_all x1, blocking collectives, shards(): parts = lax.all_to_all(partial, 'event', 0, 0, tiled=True)  19.2 us
    pallas_call x1, Pallas kernels, run_inner(): pl.pallas_call(functools.partial(inner, steps, levels, width), grid=(step...  10.2 us
    pallas_call x1, Pallas kernels, run_outer(): pl.pallas_call(functools.partial(outer, steps, levels, width), grid=(step...  6.67 us
    ppermute x1, starting transfers between devices, shards(): right = lax.ppermute(first, 'lon', [(j, i) for i, j in up])  3.84 us
    ppermute x1, starting transfers between devices, shards(): swapped = lax.ppermute(sent, 'event', swap)  3.11 us
    pallas_call x1, Pallas kernels, run_prepare(): pl.pallas_call(functools.partial(prepare, levels, width), in_specs=[pl.Bl...  1.44 us
    another operation x1, other arithmetic, shards(): jnp.stack([p_speed, s_speed, density])  1.16 us
  transfers between devices with their start and end apart: 3, of which 0 were waited for; matrix products, arithmetic and copies ran while one was open for 0% of the time, Pallas kernels for 36%

profile of v8, /device:TPU:32, one launch (start us, length us, event | category | flops | bytes accessed | tf_op | source)
XLA Modules:
  0.0 46.4 jit_solution(9410090971901443126)
XLA Ops:
  0.0 1.2 %pad_maximum_fusion.material = f32[3,16,32,128]{3,2,1,0:T(8,128)S(1)} fusion(f32[1,16,32,128]{3,2,1,0:T(8,128)} %bitcast.6, f32[1,16,32,128]{3,2,1,0:T(8,128)} %bitcast.7, f32[1,16,32,128]{3,2,1,0:T(8,128)} %bitcast.8), kind=kLoop, calls=%fused_computation | loop fusion | flops 393216 | bytes 1572864 | tf_op jit(solution)/shard_map/stack | solution.py:414
  1.2 1.4 %shard_map.55 = (bf16[12,16,8,128]{3,2,1,0:T(8,128)(2,1)S(1)}, bf16[12,16,8,128]{3,2,1,0:T(8,128)(2,1)S(1)}, bf16[9,16,32,128]{3,2,1,0:T(8,128)(2,1)S(1)}, f32[3...) custom-call(s32[1]{0:T(128)} %bitcast.row, bf16[9,16,32,128]{3,2,1,0:T(8,128)(2,1)} %bitcast.5, ...), custom_call_target="tpu_custom_call" | custom-call | tf_op jit(solution)/shard_map/pallas_call | solution.py:329
  2.6 0.1 collective-permute-start
  2.7 3.8 %collective-permute-start.1 = (bf16[12,16,8,128]{3,2,1,0:T(8,128)(2,1)S(1)}, bf16[12,16,8,128]{3,2,1,0:T(8,128)(2,1)S(1)}, u32[]{:S(2)}, u32[]{:S(2)}) collective-permute-start(bf16[12,16,8,128]{3,2,1,0:T(8,128)(2,1)S(1)} %get-tuple-element.16), channel_id=1, source_target_pairs={{1,0},{2,1},{3,2},{4,3},{5,4},{6,5},{7,6},{8,7},{9,8},{10,9},{11,1... | collective-permute-start | bytes 1179656 | tf_op jit(solution)/shard_map/ppermute | solution.py:418
  6.5 10.2 %shard_map.56 = (f32[3,16,32,128]{3,2,1,0:T(8,128)S(1)}, bf16[3,16,8,128]{3,2,1,0:T(8,128)(2,1)S(1)}, f32[3,16,8,128]{3,2,1,0:T(8,128)S(1)}, f32[2,9,16,16,128]{...) custom-call(s32[1]{0:T(128)S(6)} %select_n.5.half, bf16[9,16,32,128]{3,2,1,0:T(8,128)(2,1)S(1)} %get-tuple-element.18.init, ...), custom_call_target="tpu_custom_call" | custom-call | flops 60000000 | bytes 30000000 | tf_op jit(solution)/shard_map/pallas_call | solution.py:377
  16.7 3.1 %collective-permute-start.2 = (bf16[3,16,8,128]{3,2,1,0:T(8,128)(2,1)S(1)}, bf16[3,16,8,128]{3,2,1,0:T(8,128)(2,1)S(1)}, u32[]{:S(2)}, u32[]{:S(2)}) collective-permute-start(bf16[3,16,8,128]{3,2,1,0:T(8,128)(2,1)S(1)} %get-tuple-element.23), channel_id=1, source_target_pairs={{0,128},{16,144},{32,160},{48,176},{64,192},{80,208},{96,224},{112... | collective-permute-start | bytes 294920 | tf_op jit(solution)/shard_map/ppermute | solution.py:422
  19.8 0.0 collective-permute-done.left
  19.8 0.0 collective-permute-done.1.right
  19.8 6.7 %shard_map.57.ends = f32[2,3,16,8,128]{4,3,2,1,0:T(8,128)S(1)} custom-call(bf16[12,16,8,128]{3,2,1,0:T(8,128)(2,1)S(1)} %collective-permute-done.left, bf16[12,16,8,128]{3,2,1,0:T(8,128)(2,1)S(1)} %collective-permute-done.1.right, f32[3,16,32,128]{3,2,1,0:T(8,128)S(1)} %get-tuple-element.17.coef, bf16[8,9,16,32,128]{4,3,2,1,0:T(8,128)(2,1)S(1)} %get-tuple-element.19.forward, ...), custom_call_target="tpu_custom_call" | custom-call | flops 30000000 | bytes 20000000 | tf_op jit(solution)/shard_map/pallas_call | solution.py:394
  26.5 0.0 collective-permute-done.2.swapped
  26.5 0.1 shard_map.58
  26.6 19.2 %all_to_all.5.parts = bf16[16,3,24,128]{3,2,1,0:T(8,128)(2,1)S(1)} all-to-all(bf16[16,3,24,128]{3,2,1,0:T(8,128)(2,1)S(1)} %shard_map.58), channel_id=1, replica_groups=mesh['event'=16,'lon'=16] {'event'}, dimensions={0} | all-to-all | bytes 589824 | tf_op jit(solution)/shard_map/all_to_all | solution.py:425
  45.8 0.7 %shard_map.59 = f32[3,1,32,128]{3,2,1,0:T(8,128)} custom-call(bf16[16,3,24,128]{3,2,1,0:T(8,128)(2,1)S(1)} %all_to_all.5.parts, f32[3,32,128]{2,1,0:T(8,128)S(1)} %get-tuple-element.24.own), custom_call_target="tpu_custom_call" | custom-call | tf_op jit(solution)/shard_map/pallas_call | solution.py:359
Async XLA Ops:
  2.6 17.2 %collective-permute-start = (bf16[12,16,8,128]{3,2,1,0:T(8,128)(2,1)S(1)}, bf16[12,16,8,128]{3,2,1,0:T(8,128)(2,1)S(1)}, u32[]{:S(2)}, u32[]{:S(2)}) collective-permute-start(bf16[12,16,8,128]{3,2,1,0:T(8,128)(2,1)S(1)} %get-tuple-element.15), channel_id=1, source_target_pairs={{0,1},{1,2},{2,3},{3,4},{4,5},{5,6},{6,7},{7,8},{8,9},{9,10},{10,1... | collective-permute-start | bytes 1179656 | tf_op jit(solution)/shard_map/ppermute | solution.py:417
  2.7 17.1 %collective-permute-start.1 = (bf16[12,16,8,128]{3,2,1,0:T(8,128)(2,1)S(1)}, bf16[12,16,8,128]{3,2,1,0:T(8,128)(2,1)S(1)}, u32[]{:S(2)}, u32[]{:S(2)}) collective-permute-start(bf16[12,16,8,128]{3,2,1,0:T(8,128)(2,1)S(1)} %get-tuple-element.16), channel_id=1, source_target_pairs={{1,0},{2,1},{3,2},{4,3},{5,4},{6,5},{7,6},{8,7},{9,8},{10,9},{11,1... | collective-permute-start | bytes 1179656 | tf_op jit(solution)/shard_map/ppermute | solution.py:418
  16.7 9.8 %collective-permute-start.2 = (bf16[3,16,8,128]{3,2,1,0:T(8,128)(2,1)S(1)}, bf16[3,16,8,128]{3,2,1,0:T(8,128)(2,1)S(1)}, u32[]{:S(2)}, u32[]{:S(2)}) collective-permute-start(bf16[3,16,8,128]{3,2,1,0:T(8,128)(2,1)S(1)} %get-tuple-element.23), channel_id=1, source_target_pairs={{0,128},{16,144},{32,160},{48,176},{64,192},{80,208},{96,224},{112... | collective-permute-start | bytes 294920 | tf_op jit(solution)/shard_map/ppermute | solution.py:422

commit v9 on v8

--- a/solution.py
+++ b/solution.py
@@ -151,13 +151,11 @@
             keep(level, 0, field, step + 1, state[field, level + 1, pl.ds(PAD + step + 1, 1)])
             keep(level, 1, field, 14 - step, state[field, level + 1, pl.ds(PAD + 30 - step, 1)])
 
+    for level in range(levels):
+        velocity(level)
     for group, begin in enumerate(starts):
         pl.when(step == begin)(fetch(group).wait)
-
-    velocity(0)
     for level in range(levels):
-        if level + 1 < levels:
-            velocity(level + 1)
         stress(level)
 
     @pl.when(step == steps - 1)

time: 46.6 us -> 46.3 us (level)
  no operation moved by 1% of the time
where the time goes in v9:
time: 46.3 us; the launch traced here: 46.1 us
  blocking collectives  19.2 us (41%)
  Pallas kernels  18.7 us (40%)
  starting transfers between devices  7.04 us (15%)
  other arithmetic  1.16 us (3%)
    all_to_all x1, blocking collectives, shards(): parts = lax.all_to_all(partial, 'event', 0, 0, tiled=True)  19.2 us
    pallas_call x1, Pallas kernels, run_inner(): pl.pallas_call(functools.partial(inner, steps, levels, width), grid=(step...  9.85 us
    pallas_call x1, Pallas kernels, run_outer(): pl.pallas_call(functools.partial(outer, steps, levels, width), grid=(step...  6.67 us
    ppermute x1, starting transfers between devices, shards(): right = lax.ppermute(first, 'lon', [(j, i) for i, j in up])  3.84 us
    ppermute x1, starting transfers between devices, shards(): swapped = lax.ppermute(sent, 'event', swap)  3.11 us
    pallas_call x1, Pallas kernels, run_prepare(): pl.pallas_call(functools.partial(prepare, levels, width), in_specs=[pl.Bl...  1.44 us
    another operation x1, other arithmetic, shards(): jnp.stack([p_speed, s_speed, density])  1.16 us
  transfers between devices with their start and end apart: 3, of which 0 were waited for; matrix products, arithmetic and copies ran while one was open for 0% of the time, Pallas kernels for 36%

profile of v9, /device:TPU:32, one launch (start us, length us, event | category | flops | bytes accessed | tf_op | source)
XLA Modules:
  0.0 46.1 jit_solution(8874598224301702190)
XLA Ops:
  0.0 1.2 %pad_maximum_fusion.material = f32[3,16,32,128]{3,2,1,0:T(8,128)S(1)} fusion(f32[1,16,32,128]{3,2,1,0:T(8,128)} %bitcast.6, f32[1,16,32,128]{3,2,1,0:T(8,128)} %bitcast.7, f32[1,16,32,128]{3,2,1,0:T(8,128)} %bitcast.8), kind=kLoop, calls=%fused_computation | loop fusion | flops 393216 | bytes 1572864 | tf_op jit(solution)/shard_map/stack | solution.py:412
  1.2 1.4 %shard_map.55 = (bf16[12,16,8,128]{3,2,1,0:T(8,128)(2,1)S(1)}, bf16[12,16,8,128]{3,2,1,0:T(8,128)(2,1)S(1)}, bf16[9,16,32,128]{3,2,1,0:T(8,128)(2,1)S(1)}, f32[3...) custom-call(s32[1]{0:T(128)} %bitcast.row, bf16[9,16,32,128]{3,2,1,0:T(8,128)(2,1)} %bitcast.5, ...), custom_call_target="tpu_custom_call" | custom-call | tf_op jit(solution)/shard_map/pallas_call | solution.py:327
  2.6 0.1 collective-permute-start
  2.7 3.8 %collective-permute-start.1 = (bf16[12,16,8,128]{3,2,1,0:T(8,128)(2,1)S(1)}, bf16[12,16,8,128]{3,2,1,0:T(8,128)(2,1)S(1)}, u32[]{:S(2)}, u32[]{:S(2)}) collective-permute-start(bf16[12,16,8,128]{3,2,1,0:T(8,128)(2,1)S(1)} %get-tuple-element.16), channel_id=1, source_target_pairs={{1,0},{2,1},{3,2},{4,3},{5,4},{6,5},{7,6},{8,7},{9,8},{10,9},{11,1... | collective-permute-start | bytes 1179656 | tf_op jit(solution)/shard_map/ppermute | solution.py:416
  6.5 9.9 %shard_map.56 = (f32[3,16,32,128]{3,2,1,0:T(8,128)S(1)}, bf16[3,16,8,128]{3,2,1,0:T(8,128)(2,1)S(1)}, f32[3,16,8,128]{3,2,1,0:T(8,128)S(1)}, f32[2,9,16,16,128]{...) custom-call(s32[1]{0:T(128)S(6)} %select_n.5.half, bf16[9,16,32,128]{3,2,1,0:T(8,128)(2,1)S(1)} %get-tuple-element.18.init, ...), custom_call_target="tpu_custom_call" | custom-call | flops 60000000 | bytes 30000000 | tf_op jit(solution)/shard_map/pallas_call | solution.py:375
  16.4 3.1 %collective-permute-start.2 = (bf16[3,16,8,128]{3,2,1,0:T(8,128)(2,1)S(1)}, bf16[3,16,8,128]{3,2,1,0:T(8,128)(2,1)S(1)}, u32[]{:S(2)}, u32[]{:S(2)}) collective-permute-start(bf16[3,16,8,128]{3,2,1,0:T(8,128)(2,1)S(1)} %get-tuple-element.23), channel_id=1, source_target_pairs={{0,128},{16,144},{32,160},{48,176},{64,192},{80,208},{96,224},{112... | collective-permute-start | bytes 294920 | tf_op jit(solution)/shard_map/ppermute | solution.py:420
  19.5 0.0 collective-permute-done.left
  19.5 0.0 collective-permute-done.1.right
  19.5 6.7 %shard_map.57.ends = f32[2,3,16,8,128]{4,3,2,1,0:T(8,128)S(1)} custom-call(bf16[12,16,8,128]{3,2,1,0:T(8,128)(2,1)S(1)} %collective-permute-done.left, bf16[12,16,8,128]{3,2,1,0:T(8,128)(2,1)S(1)} %collective-permute-done.1.right, f32[3,16,32,128]{3,2,1,0:T(8,128)S(1)} %get-tuple-element.17.coef, bf16[8,9,16,32,128]{4,3,2,1,0:T(8,128)(2,1)S(1)} %get-tuple-element.19.forward, ...), custom_call_target="tpu_custom_call" | custom-call | flops 30000000 | bytes 20000000 | tf_op jit(solution)/shard_map/pallas_call | solution.py:392
  26.2 0.0 collective-permute-done.2.swapped
  26.2 0.1 shard_map.58
  26.3 19.2 %all_to_all.5.parts = bf16[16,3,24,128]{3,2,1,0:T(8,128)(2,1)S(1)} all-to-all(bf16[16,3,24,128]{3,2,1,0:T(8,128)(2,1)S(1)} %shard_map.58), channel_id=1, replica_groups=mesh['event'=16,'lon'=16] {'event'}, dimensions={0} | all-to-all | bytes 589824 | tf_op jit(solution)/shard_map/all_to_all | solution.py:423
  45.4 0.7 %shard_map.59 = f32[3,1,32,128]{3,2,1,0:T(8,128)} custom-call(bf16[16,3,24,128]{3,2,1,0:T(8,128)(2,1)S(1)} %all_to_all.5.parts, f32[3,32,128]{2,1,0:T(8,128)S(1)} %get-tuple-element.24.own), custom_call_target="tpu_custom_call" | custom-call | tf_op jit(solution)/shard_map/pallas_call | solution.py:357
Async XLA Ops:
  2.6 16.9 %collective-permute-start = (bf16[12,16,8,128]{3,2,1,0:T(8,128)(2,1)S(1)}, bf16[12,16,8,128]{3,2,1,0:T(8,128)(2,1)S(1)}, u32[]{:S(2)}, u32[]{:S(2)}) collective-permute-start(bf16[12,16,8,128]{3,2,1,0:T(8,128)(2,1)S(1)} %get-tuple-element.15), channel_id=1, source_target_pairs={{0,1},{1,2},{2,3},{3,4},{4,5},{5,6},{6,7},{7,8},{8,9},{9,10},{10,1... | collective-permute-start | bytes 1179656 | tf_op jit(solution)/shard_map/ppermute | solution.py:415
  2.7 16.8 %collective-permute-start.1 = (bf16[12,16,8,128]{3,2,1,0:T(8,128)(2,1)S(1)}, bf16[12,16,8,128]{3,2,1,0:T(8,128)(2,1)S(1)}, u32[]{:S(2)}, u32[]{:S(2)}) collective-permute-start(bf16[12,16,8,128]{3,2,1,0:T(8,128)(2,1)S(1)} %get-tuple-element.16), channel_id=1, source_target_pairs={{1,0},{2,1},{3,2},{4,3},{5,4},{6,5},{7,6},{8,7},{9,8},{10,9},{11,1... | collective-permute-start | bytes 1179656 | tf_op jit(solution)/shard_map/ppermute | solution.py:416
  16.4 9.8 %collective-permute-start.2 = (bf16[3,16,8,128]{3,2,1,0:T(8,128)(2,1)S(1)}, bf16[3,16,8,128]{3,2,1,0:T(8,128)(2,1)S(1)}, u32[]{:S(2)}, u32[]{:S(2)}) collective-permute-start(bf16[3,16,8,128]{3,2,1,0:T(8,128)(2,1)S(1)} %get-tuple-element.23), channel_id=1, source_target_pairs={{0,128},{16,144},{32,160},{48,176},{64,192},{80,208},{96,224},{112... | collective-permute-start | bytes 294920 | tf_op jit(solution)/shard_map/ppermute | solution.py:420
